TPU v7x, 256 devices: a whole 4x4x8 slice. The times are simulated.
256 devices in a mesh: pb: 8 (over y_lo, x), ia: 32 (over y_hi, z, core).
Axes of the slice: x: 4, y: 4 (y_hi: 2, y_lo: 2; y = y_hi * 2 + y_lo), z: 8, core: 2. Of those that a mesh axis runs over, the one named last changes fastest.
Arguments:
- query_feats: float32 [65536, 256], P(('pb', 'ia')), may hold values from -6 to 6
- item_table: float32 [16384, 256], P('pb'), may hold values from -6 to 6
- serve_ids: int32 [8, 32, 8, 512], P('pb', 'ia'), may hold values from 0 to 2047, as said below
- block_counts: int32 [8, 32, 8], P('pb', 'ia'), may hold values from 1 to 4, as said below
- item_refs: int32 [65536, 8], P(('pb', 'ia')), may hold values from 0 to 4095, as said below
- positive: int32 [65536], P(('pb', 'ia')), may hold values from 0 to 8191
- query_inner: float32 [256, 512], replicated, may hold values from -0.375 to 0.375
- query_outer: float32 [512, 256], replicated, may hold values from -0.25 to 0.25
- item_inner: float32 [256, 512], replicated, may hold values from -0.375 to 0.375
- item_outer: float32 [512, 256], replicated, may hold values from -0.25 to 0.25
Outputs:
- query_loss: float32 [65536], P(('pb', 'ia'))
- query_grad: float32 [65536, 256], P(('pb', 'ia'))
- table_grad: float32 [16384, 256], P(('pb', 'ia'))
Inputs may be any that keep to these rules, and one draw needn't show every extreme that they name: serve_ids[o, j, p, c] is a row of pb shard o of the table, counted from the shard's first row; the 512 rows of one list are distinct. block_counts[p, j, o] is the number of leading 128-row blocks of list serve_ids[o, j, p] that are used; in every draw some list uses all 4 blocks. `item_refs`: an entry of an item on device (p, j) is o * 512 + c with c < 128 * block_counts[p, j, o].
All inputs are finite; a program needn't handle non-finite values.
Results may differ from a plain program's by a relative error of at most 0.00029.
Values sent between devices are 32-bit elements; how exact they have to be, the bound alone decides.
A program may use at most 128 MiB of HBM per device.

v0:
```python
import jax
import jax.numpy as jnp
from jax import lax
from jax.sharding import PartitionSpec as P

BLOCK = 128


inverse_temp = 20.0
epsilon = 1e-06
highest = lax.Precision.HIGHEST


def matmul(left, right):
    return jnp.dot(left, right, preferred_element_type=jnp.float32, precision=highest)


def matmul_nt(left, right):
    return lax.dot_general(
        left, right, (((1,), (1,)), ((), ())), precision=highest, preferred_element_type=jnp.float32
    )


def matmul_tn(left, right):
    return lax.dot_general(
        left, right, (((0,), (0,)), ((), ())), precision=highest, preferred_element_type=jnp.float32
    )


def normalize(raw_rows):
    return raw_rows * lax.rsqrt(jnp.sum(raw_rows * raw_rows, axis=1, keepdims=True) + epsilon)


def query_tower(features, query_inner, query_outer):
    return normalize(
        matmul(jax.nn.gelu(matmul(features, query_inner), approximate=False), query_outer)
    )


def item_head(pooled, item_outer):
    return normalize(matmul(pooled, item_outer))


def per_device(
    query_feats,
    item_table,
    serve_ids,
    block_counts,
    item_refs,
    positive,
    query_inner,
    query_outer,
    item_inner,
    item_outer,
):
    owners = lax.axis_size("pb")
    row_lists = serve_ids[0, 0]
    capacity = row_lists.shape[1]
    counts = block_counts[0, 0]
    outgoing = item_table[row_lists]
    incoming = lax.all_to_all(outgoing, "pb", split_axis=0, concat_axis=0, tiled=True)
    valid_rows = (jnp.arange(capacity, dtype=jnp.int32)[None, :] < BLOCK * counts[:, None]).reshape(
        -1
    )
    slot_feats = jnp.where(
        valid_rows[:, None], incoming.reshape(owners * capacity, incoming.shape[2]), 0.0
    )
    pre_act = matmul(slot_feats, item_inner)
    slot_hidden, gelu_back = jax.vjp(lambda inputs: jax.nn.gelu(inputs, approximate=False), pre_act)
    rows_here = item_refs.shape[0]
    refs_each = item_refs.shape[1]
    hidden_width = slot_hidden.shape[1]
    flat_refs = item_refs.reshape(-1)
    pooled = jnp.sum(slot_hidden[flat_refs].reshape(rows_here, refs_each, hidden_width), axis=1)
    item_emb, head_back = jax.vjp(lambda inputs: item_head(inputs, item_outer), pooled)
    query_emb, query_back = jax.vjp(
        lambda inputs: query_tower(inputs, query_inner, query_outer), query_feats
    )
    block_items = lax.all_gather(item_emb, "ia", axis=0, tiled=True)
    row_count = block_items.shape[0]
    weights_exp = jnp.exp(inverse_temp * matmul_nt(query_emb, block_items))
    inside = (positive >= 0) & (positive < row_count)
    picked = block_items[jnp.clip(positive, 0, row_count - 1)]
    sum_exp = jnp.sum(weights_exp, axis=1)
    weighted = matmul(weights_exp, block_items)
    positive_emb = jnp.where(inside[:, None], picked, 0.0)
    log_total = jnp.log(sum_exp)
    query_loss = log_total - inverse_temp * jnp.sum(query_emb * positive_emb, axis=1)
    grad_query_emb = inverse_temp * (weighted / sum_exp[:, None] - positive_emb)
    query_grad = query_back(grad_query_emb)[0]
    my_index = (lax.axis_index("ia") * rows_here + jnp.arange(rows_here, dtype=jnp.int32)).astype(
        jnp.float32
    )
    block_queries = lax.all_gather(query_emb, "ia", axis=0, tiled=True)
    block_total = lax.all_gather(log_total, "ia", axis=0, tiled=True)
    block_positive = lax.all_gather(positive.astype(jnp.float32), "ia", axis=0, tiled=True)
    probability = jnp.exp(inverse_temp * matmul_nt(block_queries, item_emb) - block_total[:, None])
    coefficient = probability - (block_positive[:, None] == my_index[None, :]).astype(jnp.float32)
    grad_item_emb = inverse_temp * matmul_tn(coefficient, block_queries)
    grad_pooled = head_back(grad_item_emb)[0]
    spread = jnp.broadcast_to(
        grad_pooled[:, None, :], (rows_here, refs_each, hidden_width)
    ).reshape(rows_here * refs_each, hidden_width)
    grad_hidden = jax.ops.segment_sum(spread, flat_refs, num_segments=slot_feats.shape[0])
    grad_pre = gelu_back(grad_hidden)[0]
    grad_slots = matmul_nt(grad_pre, item_inner)
    grad_slots = jnp.where(valid_rows[:, None], grad_slots, 0.0)
    grad_lists = grad_slots.reshape(owners, capacity, grad_slots.shape[1])
    returned = lax.all_to_all(grad_lists, "pb", split_axis=0, concat_axis=0, tiled=True)
    local_grad = (
        jnp.zeros(item_table.shape, jnp.float32)
        .at[row_lists.reshape(-1)]
        .add(returned.reshape(owners * capacity, returned.shape[2]))
    )
    table_grad = lax.psum_scatter(local_grad, "ia", scatter_dimension=0, tiled=True)
    return (query_loss, query_grad, table_grad)


def solution(mesh):
    placed = (
        P(("pb", "ia"), None),
        P("pb", None),
        P("pb", "ia", None, None),
        P("pb", "ia", None),
        P(("pb", "ia"), None),
        P(("pb", "ia")),
        P(),
        P(),
        P(),
        P(),
    )
    return jax.shard_map(
        per_device,
        mesh=mesh,
        in_specs=placed,
        out_specs=(P(("pb", "ia")), P(("pb", "ia"), None), P(("pb", "ia"), None)),
        check_vma=False,
    )
```

profile of v0, /device:TPU:1, one launch (start us, length us, event | category | flops | bytes accessed | tf_op | source)
XLA Modules:
  0.0 643.9 jit_solution(11231752377565032626)
XLA Ops:
  7.2 0.9 fusion.68
  8.8 16.1 %gather_fusion = f32[4096,256]{1,0:T(8,128)} fusion(f32[2048,256]{1,0:T(8,128)S(1)} %copy-done, s32[4096]{0:T(1024)S(1)} %broadcast_clamp_fusion), kind=kCustom, calls=%fused_computation | custom fusion | bytes 8404992 | tf_op jit(solution)/shard_map/gather | solution.py:60
  24.9 6.0 all-to-all-start
  31.3 49.2 %all-to-all-done = f32[8,512,256]{2,1,0:T(8,128)} async-done(((f32[8,512,256]{2,1,0:T(8,128)}), f32[8,512,256]{2,1,0:T(8,128)}, u32[]{:S(2)}, u32[]{:S(2)}) %all-to-all-start) | async-done | bytes 4194336 | tf_op jit(solution)/shard_map/all_to_all | solution.py:61
  80.5 4.1 bitcast_select_fusion
  84.6 26.8 %multiply_multiply_fusion.5 = (f32[4096,512]{1,0:T(8,128)}, f32[4096,512]{1,0:T(8,128)}, f32[4096,512]{1,0:T(8,128)}) fusion(f32[4096,256]{1,0:T(8,128)S(1)} %bitcast_select_fusion, f32[256,512]{1,0:T(8,128)S(1)} %copy-done.15), kind=kOutput, calls=%fused_computation.37 | convolution fusion | flops 6576668672 | bytes 29884416 | tf_op jit(solution)/shard_map/dot_general | solution.py:15
  111.4 13.0 %gather_fusion.1 = f32[2048,512]{1,0:T(8,128)} fusion(f32[4096,512]{1,0:T(8,128)} %get-tuple-element.5, s32[2048]{0:T(1024)S(1)} %broadcast_clamp_fusion.1), kind=kCustom, calls=%fused_computation.1 | custom fusion | bytes 8396800 | tf_op jit(solution)/shard_map/gather | solution.py:74
  124.4 3.3 bitcast_reduce_fusion
  127.8 1.0 multiply_reduce_fusion.3
  128.8 0.7 broadcast_multiply_fusion
  129.7 1.7 fusion.34
  131.4 1.0 multiply_reduce_fusion.4
  132.4 120.8 %all-gather.5.cloned.1.call-done = f32[8192,256]{0,1:T(8,128)} async-done(((f32[256,256]{0,1:T(8,128)}), f32[8192,256]{0,1:T(8,128)}) %all-gather.5.cloned.1.call-update) | async-done | bytes 8388624 | tf_op jit(solution)/shard_map/all_gather | solution.py:79
  253.2 9.0 %copy.20 = f32[8192,256]{1,0:T(8,128)} copy(f32[8192,256]{0,1:T(8,128)} %all-gather.5.cloned.1.call-done) | data formatting | bytes 16777216 | tf_op jit(solution)/shard_map/all_gather | solution.py:79
  262.2 4.3 gather_fusion.2
  266.7 0.7 multiply_reduce_fusion.2
  267.6 39.6 %all-gather.1 = f32[32,1,256]{2,1,0:T(1,128)S(1)} all-gather(f32[1,1,256]{2,1,0:T(1,128)S(1)} %bitcast.60), channel_id=1, replica_groups=mesh['pb'=8,'ia'=32] {'ia'}, dimensions={0}, use_global_device_ids=true | all-gather | bytes 33792 | tf_op jit(solution)/shard_map/all_gather | solution.py:96
  307.2 12.8 %fusion.80 = (f32[256]{0:T(256)S(1)}, f32[256,8192]{1,0:T(8,128)}) fusion(f32[256,256]{0,1:T(8,128)} %get-tuple-element.4, f32[8192,256]{0,1:T(8,128)} %all-gather.5.cloned.1.call-done), kind=kOutput, calls=%fused_computation.133 | convolution fusion | flops 6446645248 | bytes 17040384 | tf_op jit(solution)/shard_map/dot_general | solution.py:19
  320.5 36.7 %all-gather = f32[32,1,256]{2,1,0:T(1,128)S(1)} all-gather(f32[1,1,256]{2,1,0:T(1,128)S(1)} %bitcast.61), channel_id=1, replica_groups=mesh['pb'=8,'ia'=32] {'ia'}, dimensions={0}, use_global_device_ids=true | all-gather | bytes 33792 | tf_op jit(solution)/shard_map/all_gather | solution.py:95
  357.2 15.2 %all-gather.7.cloned.1.call-done = f32[8192,256]{0,1:T(8,128)} async-done(((f32[256,256]{0,1:T(8,128)}), f32[8192,256]{0,1:T(8,128)}) %all-gather.7.cloned.1.call-update) | async-done | bytes 8388624 | tf_op jit(solution)/shard_map/all_gather | solution.py:94
  372.4 19.0 %fusion.3 = f32[8192,256]{1,0:T(8,128)S(1)} fusion(f32[8192,256]{0,1:T(8,128)} %all-gather.7.cloned.1.call-done, f32[256,256]{0,1:T(8,128)S(1)} %copy-done.3, f32[256]{0:T(256)S(1)} %add_convert_fusion, f32[8192]{0:T(1024)S(1)} %bitcast.53, f32[8192]{0:T(1024)S(1)} %bitcast.52), kind=kOutput, calls=%fused_computation.11 | convolution fusion | flops 6452936704 | bytes 17105920 | tf_op jit(solution)/shard_map/dot_general | solution.py:19
  391.4 7.4 %multiply_reduce_fusion = (f32[256]{0:T(256)S(1)}, f32[256,256]{0,1:T(8,128)S(1)}) fusion(f32[256,256]{0,1:T(8,128)S(1)} %get-tuple-element.17, f32[8192,256]{1,0:T(8,128)S(1)} %fusion.3, f32[8192,256]{0,1:T(8,128)S(1)} %copy-done.2), kind=kOutput, calls=%fused_computation.86 | convolution fusion | flops 6442647552 | bytes 17302528 | tf_op jit(solution)/shard_map/dot_general | solution.py:25
  398.8 1.1 fusion.55
  399.8 16.5 %scatter_custom_fusion = f32[4096,512]{1,0:T(8,128)} fusion(s32[2048]{0:T(1024)S(1)} %reshape.199, f32[]{:T(128)} %constant.52.clone.1, f32[256,512]{1,0:T(8,128)S(1)} %fusion.55), kind=kCustom, calls=%fused_computation.39 | custom fusion | flops 1048576 | bytes 8912900 | tf_op jit(solution)/shard_map/scatter-add | solution.py:104
  416.3 18.2 %fusion.21 = f32[4096,256]{1,0:T(8,128)} fusion(f32[256,512]{1,0:T(8,128)} %param.18, f32[4096,512]{1,0:T(8,128)} %scatter_custom_fusion, f32[4096,512]{1,0:T(8,128)} %get-tuple-element.6, f32[4096,512]{1,0:T(8,128)} %get-tuple-element.15, pred[4096]{0:T(1024)(128)(4,1)S(1)} %bitcast.58), kind=kOutput, calls=%fused_computation.38 | convolution fusion | flops 6470762496 | bytes 29888512 | tf_op jit(solution)/shard_map/dot_general | solution.py:19
  434.5 4.7 all-to-all-start.1
  439.4 49.5 %all-to-all-done.1 = f32[8,512,256]{2,1,0:T(8,128)} async-done(((f32[8,512,256]{2,1,0:T(8,128)}), f32[8,512,256]{2,1,0:T(8,128)}, u32[]{:S(2)}, u32[]{:S(2)}) %all-to-all-start.1) | async-done | bytes 4194336 | tf_op jit(solution)/shard_map/all_to_all | solution.py:109
  488.9 24.3 %scatter_custom_fusion.1 = f32[2048,256]{1,0:T(8,128)} fusion(s32[4096]{0:T(1024)S(1)} %bitcast.59, f32[4096,256]{1,0:T(8,128)} %bitcast.13, f32[]{:T(128)} %constant.52.clone.1), kind=kCustom, calls=%fused_computation.50 | custom fusion | flops 1048576 | bytes 2097664 | tf_op jit(solution)/shard_map/scatter-add | solution.py:113
  513.2 11.0 %multiply_reduce_fusion.1 = (f32[256]{0:T(256)S(1)}, f32[256,256]{0,1:T(8,128)S(1)}) fusion(f32[256,256]{0,1:T(8,128)S(1)} %get-tuple-element.21, f32[256,256]{0,1:T(8,128)S(1)} %copy.21, pred[256]{0:T(512)(128)(4,1)S(1)} %compare_and_fusion, f32[256]{0:T(256)S(1)} %get-tuple-element.22, f32[256,8192]{1,0:T(8,128)} %get-tuple-element.23, ...), kind=kOutput, calls=%fused_computation.90 | convolution fusion | flops 6442844160 | bytes 17565952 | tf_op jit(solution)/shard_map/dot_general | solution.py:15
  524.2 1.1 fusion.54
  525.3 1.5 fusion.35
  526.8 110.1 %reduce-scatter.2.cloned.1.call-done = f32[64,256]{1,0:T(8,128)} async-done(((f32[2048,256]{1,0:T(8,128)}), f32[64,256]{1,0:T(8,128)}) %reduce-scatter.2.cloned.1.call-update) | async-done | bytes 65552 | tf_op jit(solution)/shard_map/reduce_scatter | solution.py:115
  (64 shorter events, 2.2 us)
Async XLA Ops:
  7.2 1.6 copy-start
  24.9 6.1 copy-start.17
  24.9 6.2 copy-start.13
  24.9 59.7 %copy-start.15 = (f32[256,512]{1,0:T(8,128)S(1)}, f32[256,512]{1,0:T(8,128)}, u32[]{:S(2)}) copy-start(f32[256,512]{1,0:T(8,128)} %param.18) | copy-start | bytes 1572868
  24.9 55.6 %all-to-all-start = ((f32[8,512,256]{2,1,0:T(8,128)}), f32[8,512,256]{2,1,0:T(8,128)}, u32[]{:S(2)}, u32[]{:S(2)}) async-start(f32[8,512,256]{2,1,0:T(8,128)} %bitcast.50), calls=%async_computation | async-start | bytes 8388608 | tf_op jit(solution)/shard_map/all_to_all | solution.py:61
  30.9 222.3 %all-gather.5.cloned.1.call-start = ((), (), s32[]{:S(2)}) async-start(), calls=%async_computation.3 | async-start | bytes 8650752 | tf_op jit(solution)/shard_map/all_gather | solution.py:79
  111.4 16.3 %copy-start.5 = (f32[512,256]{1,0:T(8,128)S(1)}, f32[512,256]{1,0:T(8,128)}, u32[]{:S(2)}) copy-start(f32[512,256]{1,0:T(8,128)} %param.19) | copy-start | bytes 1572868
  111.4 18.2 %copy-start.14 = (s32[256]{0:T(256)S(1)}, s32[256]{0:T(256)}, u32[]{:S(2)}) copy-start(s32[256]{0:T(256)} %param.15) | copy-start | bytes 3076
  111.4 18.2 %copy-start.10 = (f32[256,512]{1,0:T(8,128)S(1)}, f32[256,512]{1,0:T(8,128)}, u32[]{:S(2)}) copy-start(f32[256,512]{1,0:T(8,128)} %param.16) | copy-start | bytes 1572868
  111.4 18.2 %copy-start.16 = (f32[256,256]{1,0:T(8,128)S(1)}, f32[256,256]{1,0:T(8,128)}, u32[]{:S(2)}) copy-start(f32[256,256]{1,0:T(8,128)} %param.10) | copy-start | bytes 786436
  124.4 6.9 %copy-start.4 = (f32[512,256]{1,0:T(8,128)S(1)}, f32[512,256]{1,0:T(8,128)}, u32[]{:S(2)}) copy-start(f32[512,256]{1,0:T(8,128)} %param.17) | copy-start | bytes 1572868
  129.5 242.9 %all-gather.7.cloned.1.call-start = ((), (), s32[]{:S(2)}) async-start(), calls=%async_computation.4 | async-start | bytes 8650752 | tf_op jit(solution)/shard_map/all_gather | solution.py:94
  131.3 130.8 %copy-start.6 = (f32[256,512]{1,0:T(8,128)}, f32[256,512]{1,0:T(8,128)S(1)}, u32[]{:S(2)}) copy-start(f32[256,512]{1,0:T(8,128)S(1)} %get-tuple-element.18) | copy-start | bytes 1572868
  131.3 130.8 %copy-start.8 = (f32[256,512]{1,0:T(8,128)}, f32[256,512]{1,0:T(8,128)S(1)}, u32[]{:S(2)}) copy-start(f32[256,512]{1,0:T(8,128)S(1)} %get-tuple-element.19) | copy-start | bytes 1572868
  307.2 65.2 %copy-start.3 = (f32[256,256]{0,1:T(8,128)S(1)}, f32[256,256]{0,1:T(8,128)}, u32[]{:S(2)}) copy-start(f32[256,256]{0,1:T(8,128)} %broadcast_multiply_fusion) | copy-start | bytes 786436
  372.4 19.0 %copy-start.2 = (f32[8192,256]{0,1:T(8,128)S(1)}, f32[8192,256]{0,1:T(8,128)}, u32[]{:S(2)}) copy-start(f32[8192,256]{0,1:T(8,128)} %all-gather.7.cloned.1.call-done) | copy-start | bytes 25165828
  434.5 4.7 copy-start.12
  434.5 54.3 %all-to-all-start.1 = ((f32[8,512,256]{2,1,0:T(8,128)}), f32[8,512,256]{2,1,0:T(8,128)}, u32[]{:S(2)}, u32[]{:S(2)}) async-start(f32[8,512,256]{2,1,0:T(8,128)} %bitcast.51), calls=%async_computation.1 | async-start | bytes 8388608 | tf_op jit(solution)/shard_map/all_to_all | solution.py:109
  439.2 197.7 %reduce-scatter.2.cloned.1.call-start = ((), (), s32[]{:S(2)}) async-start(), calls=%async_computation.5 | async-start | bytes 2162688 | tf_op jit(solution)/shard_map/reduce_scatter | solution.py:115
  513.2 123.7 %copy-start.1 = (f32[2048,256]{1,0:T(8,128)S(1)}, f32[2048,256]{1,0:T(8,128)}, u32[]{:S(2)}) copy-start(f32[2048,256]{1,0:T(8,128)} %param.11) | copy-start | bytes 6291460
  513.2 12.1 %copy-start.7 = (f32[256,512]{1,0:T(8,128)S(1)}, f32[256,512]{1,0:T(8,128)}, u32[]{:S(2)}) copy-start(f32[256,512]{1,0:T(8,128)} %copy-done.6) | copy-start | bytes 1572868
  513.2 12.1 %copy-start.9 = (f32[256,512]{1,0:T(8,128)S(1)}, f32[256,512]{1,0:T(8,128)}, u32[]{:S(2)}) copy-start(f32[256,512]{1,0:T(8,128)} %copy-done.8) | copy-start | bytes 1572868
  513.2 12.1 %copy-start.11 = (f32[256,512]{1,0:T(8,128)S(1)}, f32[256,512]{1,0:T(8,128)}, u32[]{:S(2)}) copy-start(f32[256,512]{1,0:T(8,128)} %param.16) | copy-start | bytes 1572868
Sparse Core Ops, SparseCore 0:
  129.7 123.5 all-gather.4
  267.6 104.7 all-gather.6
  513.3 123.5 reduce-scatter.1
where the time goes:
time: 656 us; the launch traced here: 644 us
  waiting for transfers between devices  345 us (53%)
  matrix products  102 us (16%)
  blocking collectives  76.3 us (12%)
  other arithmetic  51.3 us (8%)
  local copies, waits for them, and re-layouts  43.7 us (7%)
  between operations  14.5 us (2%)
  starting transfers between devices  10.8 us (2%)
    all_gather x1, waiting for transfers between devices, per_device(): block_items = lax.all_gather(item_emb, 'ia', axis=0, tiled=True)  121 us
    reduce_scatter x1, waiting for transfers between devices, per_device(): lax.psum_scatter(local_grad, 'ia', scatter_dimension=0, tiled=True)  110 us
    dot_general x3, matrix products, matmul_nt(): lax.dot_general(left, right, (((1,), (1,)), ((), ())), precision=highest,...  49.9 us
    all_to_all x1, waiting for transfers between devices, per_device(): lax.all_to_all(grad_lists, 'pb', split_axis=0, concat_axis=0, tiled=True)  49.5 us
    all_to_all x1, waiting for transfers between devices, per_device(): lax.all_to_all(outgoing, 'pb', split_axis=0, concat_axis=0, tiled=True)  49.2 us
    dot_general x8, matrix products, matmul(): jnp.dot(left, right, preferred_element_type=jnp.float32, precision=highest)  45.1 us
    all_gather x1, blocking collectives, per_device(): lax.all_gather(positive.astype(jnp.float32), 'ia', axis=0, tiled=True)  39.6 us
    all_gather x1, blocking collectives, per_device(): block_total = lax.all_gather(log_total, 'ia', axis=0, tiled=True)  36.7 us
  transfers between devices with their start and end apart: 5, of which 5 were waited for; matrix products, arithmetic and copies ran while one was open for 5% of the time, Pallas kernels for 0%

commit v1 on v0

v1 whole, which is shorter than its diff:
```python
import functools

import jax
import jax.numpy as jnp
from jax import lax
from jax.experimental import pallas as pl
from jax.experimental.pallas import tpu as pltpu
from jax.sharding import PartitionSpec as P

BLOCK = 128
CAP = 512
MESH = pl.DeviceIdType.MESH
VM = pltpu.VMEM
DMA = pltpu.SemaphoreType.DMA
f32 = jnp.float32
bf16 = jnp.bfloat16

inverse_temp = 20.0
epsilon = 1e-06

NN = (((1,), (0,)), ((), ()))
NT = (((1,), (1,)), ((), ()))


def split(v):
    hi = v.astype(bf16)
    return hi, (v - hi.astype(f32)).astype(bf16)


def dot(a, b, dims=NN):
    return lax.dot_general(a, b, dims, preferred_element_type=f32)


def dot3(a, b, dims=NN):
    return dot(a[0], b[0], dims) + (dot(a[0], b[1], dims) + dot(a[1], b[0], dims))


def normal_cdf(v):
    return 0.5 * (1.0 + lax.erf(v * 0.7071067811865476))


def gelu(v):
    return v * normal_cdf(v)


def gelu_slope(v):
    return normal_cdf(v) + v * (0.3989422804014327 * jnp.exp(-0.5 * v * v))


def place():
    p, j = lax.axis_index("pb"), lax.axis_index("ia")
    return p, j, p % 4, p // 4, j // 16, (j // 2) % 8, j % 2


def greet(peers):
    barrier = pltpu.get_barrier_semaphore()
    for peer in peers:
        pl.semaphore_signal(barrier, inc=1, device_id=peer, device_id_type=MESH)
    pl.semaphore_wait(barrier, len(peers))


def push(src, dst, send, recv, peer):
    return pltpu.make_async_remote_copy(
        src_ref=src, dst_ref=dst, send_sem=send, recv_sem=recv, device_id=peer, device_id_type=MESH
    )


def pool_kernel(
    refs_ref,
    lists_ref,
    pos_ref,
    table_ref,
    inner_ref,
    outer_ref,
    qf_ref,
    qi_ref,
    qo_ref,
    raw_ref,
    qpre_ref,
    qraw_ref,
    ct_ref,
    qall_ref,
    posall_ref,
    refs_all,
    zh,
    zl,
    innh,
    innl,
    outh,
    outl,
    qemb,
    ct,
    part,
    got,
    refs_sem,
    pos_sem,
    q_sem,
    part_sem,
    ct_sem,
    own_sem,
):
    p, j, x, yl, yh, z, core = place()

    def zdev(d):
        return (p, (yh * 8 + (z + d) % 8) * 2 + core)

    def pbdev(dy, dx):
        return (((yl + dy) % 2) * 4 + (x + dx) % 4, j)

    pb_peers = [(dy, dx) for dy in range(2) for dx in range(4) if dy or dx]
    greet([pbdev(*d) for d in pb_peers] + [zdev(d) for d in range(1, 8)])

    refs_cp = [
        push(refs_ref, refs_all.at[p], refs_sem.at[0, i], refs_sem.at[1, i], pbdev(*d))
        for i, d in enumerate(pb_peers)
    ]
    pos_cp = [
        push(pos_ref, posall_ref.at[z], pos_sem.at[0, i], pos_sem.at[1, i], zdev(i + 1))
        for i in range(7)
    ]
    for c in refs_cp + pos_cp:
        c.start()
    refs_all[p] = refs_ref[...]
    own_pos = pltpu.make_async_copy(pos_ref, posall_ref.at[z], own_sem.at[0])
    own_pos.start()

    qpre = dot3(split(qf_ref[...]), split(qi_ref[...]))
    qpre_ref[...] = qpre
    qraw = dot3(split(gelu(qpre)), split(qo_ref[...]))
    qraw_ref[...] = qraw
    qemb[...] = qraw * lax.rsqrt(jnp.sum(qraw * qraw, axis=1, keepdims=True) + epsilon)
    own_q = pltpu.make_async_copy(qemb, qall_ref.at[z], own_sem.at[1])
    own_q.start()

    def right(s):
        b = (z + 8 - s) % 8
        src = qemb if s == 0 else qall_ref.at[b]
        return push(src, qall_ref.at[b], q_sem.at[0, s], q_sem.at[1, s], zdev(1))

    def left(s):
        b = (z + s) % 8
        src = qemb if s == 0 else qall_ref.at[b]
        return push(src, qall_ref.at[b], q_sem.at[0, 4 + s], q_sem.at[1, 4 + s], zdev(7))

    right(0).start()
    left(0).start()

    ih, il = split(jnp.transpose(inner_ref[...]))
    innh[...], innl[...] = ih, il
    oh, ol = split(jnp.transpose(outer_ref[...]))
    outh[...], outl[...] = oh, ol

    def rows(t, carry):
        r = pl.ds(pl.multiple_of(t * 256, 256), 256)
        hid = dot3((innh[...], innl[...]), split(table_ref[r, :]), NT)
        h, l = split(dot3((outh[...], outl[...]), split(gelu(hid))))
        zh[:, r] = h
        zl[:, r] = l
        return carry

    lax.fori_loop(0, 8, rows, 0)

    for c in refs_cp:
        c.wait()

    def piece(s):
        k = s // 2
        dx = (1 - k // 2) * (2 + k) + (k // 2) * (3 - k)
        dy = 1 - s % 2
        return pbdev(dy, dx)

    def part_cp(s):
        dest = piece(s)
        return push(part.at[s], got.at[p], part_sem.at[0, s], part_sem.at[1, s], dest)

    def ct_cp(s):
        b = piece(s)[0]
        return pltpu.make_async_copy(ct.at[b], ct_ref.at[b], ct_sem.at[s])

    def pieces(s, carry):
        b = piece(s)[0]
        refs = refs_all[b]
        slot = lax.broadcasted_iota(jnp.int32, (CAP, 256), 0) + p * CAP
        uses = jnp.zeros((CAP, 256), f32)
        for k in range(8):
            uses = uses + jnp.where(slot == refs[k : k + 1, :], 1.0, 0.0)
        uses = uses.astype(bf16)
        listed = lists_ref[pl.ds(b, 1), :]
        total = jnp.zeros((256, 256), f32)
        for t in range(8):
            row = lax.broadcasted_iota(jnp.int32, (256, CAP), 0) + t * 256
            pick = jnp.where(row == listed, 1.0, 0.0).astype(bf16)
            times = dot(pick, uses).astype(bf16)
            ct[b, t * 256 : (t + 1) * 256, :] = times
            w = slice(t * 256, (t + 1) * 256)
            total = total + (dot(zh[:, w], times) + dot(zl[:, w], times))
        ct_cp(s).start()

        @pl.when(s < 7)
        def _():
            part[s] = total
            part_cp(s).start()

        @pl.when(s == 7)
        def _():
            got[p] = total

        return carry

    lax.fori_loop(0, 3, pieces, 0)
    right(0).wait_recv()
    right(1).start()
    left(0).wait_recv()
    left(1).start()
    lax.fori_loop(3, 6, pieces, 0)
    right(1).wait_recv()
    right(2).start()
    left(1).wait_recv()
    left(2).start()
    lax.fori_loop(6, 8, pieces, 0)
    right(2).wait_recv()
    right(3).start()
    left(2).wait_recv()
    for s in range(7):
        part_cp(s).wait()
    acc = got[0]
    for b in range(1, 8):
        acc = acc + got[b]
    raw_ref[...] = jnp.transpose(acc)
    right(3).wait_recv()
    for s in range(4):
        right(s).wait_send()
    for s in range(3):
        left(s).wait_send()
    for c in pos_cp:
        c.wait()
    own_pos.wait()
    own_q.wait()
    for s in range(8):
        ct_cp(s).wait()


def loss_kernel(
    raw_ref,
    q_ref,
    pos_ref,
    loss_ref,
    draw_ref,
    dq_ref,
    items,
    qh,
    ql,
    iTh,
    iTl,
    ex,
    stats,
    stats_all,
    ditem,
    dsend,
    dgot,
    item_sem,
    stat_sem,
    d_sem,
):
    p, j, x, yl, yh, z, core = place()

    def at(dyh, dz, dc):
        return (p, (((yh + dyh) % 2) * 8 + (z + dz) % 8) * 2 + (core + dc) % 2)

    near = [(0, 1), (1, 0), (1, 1)]
    greet([at(a, 0, c) for a, c in near] + [at(0, d, 0) for d in range(1, 8)])

    raw = raw_ref[...]
    inv_norm = lax.rsqrt(jnp.sum(raw * raw, axis=1, keepdims=True) + epsilon)
    emb = raw * inv_norm
    items[0] = emb
    item_cp = [
        push(items.at[0], items.at[i + 1], item_sem.at[0, i], item_sem.at[1, i], at(a, 0, c))
        for i, (a, c) in enumerate(near)
    ]
    for i in (1, 2, 0):
        item_cp[i].start()
    for b in range(8):
        h, l = split(q_ref[b])
        qh[b], ql[b] = h, l
    stats[...] = jnp.zeros((16, 256), f32)

    def base(i):
        a, c = ([(0, 0)] + near)[i]
        return (((yh + a) % 2) * 8 + z) * 2 + (core + c) % 2

    def logits(i):
        here = items[i]
        ih, il = split(here)
        th, tl = split(jnp.transpose(here))
        iTh[i], iTl[i] = th, tl
        number = lax.broadcasted_iota(jnp.int32, (256, 256), 0) + base(i) * 256

        def step(b, carry):
            lg = inverse_temp * dot3((ih, il), (qh[b], ql[b]), NT)
            e = jnp.exp(lg)
            ex[i, b] = e
            r = pl.ds(b, 1)
            stats[r, :] = stats[r, :] + jnp.sum(e, axis=0, keepdims=True)
            hit = pos_ref[b][0:1, :] == number
            r8 = pl.ds(b + 8, 1)
            stats[r8, :] = stats[r8, :] + jnp.sum(jnp.where(hit, lg, 0.0), axis=0, keepdims=True)
            return carry

        lax.fori_loop(0, 8, step, 0)

    logits(0)
    for i in range(3):
        item_cp[i].wait_recv()
        logits(i + 1)

    stat_cp = [
        push(stats, stats_all.at[z], stat_sem.at[0, i], stat_sem.at[1, i], at(0, i + 1, 0))
        for i in range(7)
    ]
    for c in stat_cp:
        c.start()
    stats_all[z] = stats[...]
    for c in stat_cp:
        c.wait()
    both = stats_all[0]
    for b in range(1, 8):
        both = both + stats_all[b]
    stats[...] = both
    loss_ref[...] = jnp.log(stats[pl.ds(z, 1), :]) - stats[pl.ds(z + 8, 1), :]
    stats[0:8, :] = inverse_temp / both[0:8, :]

    def grads(i, first):
        number = lax.broadcasted_iota(jnp.int32, (256, 256), 0) + base(i) * 256
        th, tl = iTh[i], iTl[i]

        def step(b, total):
            hit = pos_ref[b][0:1, :] == number
            coef = ex[i, b] * stats[pl.ds(b, 1), :] - jnp.where(hit, inverse_temp, 0.0)
            c = split(coef)
            back = dot3((th, tl), c)
            if first:
                dq_ref[b] = back
            else:
                dq_ref[b] = dq_ref[b] + back
            return total + dot3(c, (qh[b], ql[b]))

        return lax.fori_loop(0, 8, step, jnp.zeros((256, 256), f32))

    to_sib = [
        push(dsend.at[i], dgot.at[i], d_sem.at[0, i], d_sem.at[1, i], at(0, 0, 1)) for i in range(2)
    ]
    across = push(dsend.at[2], dgot.at[2], d_sem.at[0, 2], d_sem.at[1, 2], at(1, 0, 0))
    dsend[0] = grads(3, True)
    to_sib[0].start()
    mine = grads(2, False)
    to_sib[0].wait_recv()
    dsend[2] = mine + dgot[0]
    across.start()
    dsend[1] = grads(1, False)
    to_sib[1].start()
    mine = grads(0, False)
    to_sib[1].wait_recv()
    mine = mine + dgot[1]
    across.wait_recv()
    d = mine + dgot[2]
    draw_ref[...] = inv_norm * (d - emb * jnp.sum(emb * d, axis=1, keepdims=True))
    for c in item_cp:
        c.wait_send()
    for c in to_sib:
        c.wait_send()
    across.wait_send()


def table_kernel(
    draw_ref,
    dq_ref,
    qpre_ref,
    qraw_ref,
    table_ref,
    inner_ref,
    outer_ref,
    qi_ref,
    qo_ref,
    ct_ref,
    qg_ref,
    tg_ref,
    d_all,
    ct,
    acc,
    csend,
    cgot,
    zsend,
    zgot,
    ysend,
    ygot,
    qsend,
    qgot,
    ct_sem,
    d_sem,
    c_sem,
    z_sem,
    y_sem,
    q_sem,
):
    p, j, x, yl, yh, z, core = place()

    def at(dyh, dz, dc):
        return (p, (((yh + dyh) % 2) * 8 + (z + dz) % 8) * 2 + (core + dc) % 2)

    def pbdev(dy, dx):
        return (((yl + dy) % 2) * 4 + (x + dx) % 4, j)

    order = [(1, 0), (0, 1), (0, 3), (0, 2), (1, 1), (1, 3), (1, 2)]
    greet([pbdev(*d) for d in order] + [at(0, 1, 0), at(0, 7, 0), at(0, 0, 1), at(1, 0, 0)])

    load = [pltpu.make_async_copy(ct_ref.at[b], ct.at[b], ct_sem.at[b]) for b in range(8)]
    for c in load:
        c.start()
    d_cp = [
        push(draw_ref, d_all.at[p], d_sem.at[0, i], d_sem.at[1, i], pbdev(*d))
        for i, d in enumerate(order)
    ]
    for c in d_cp:
        c.start()
    d_all[p] = draw_ref[...]

    def q_right(s):
        return push(qsend.at[s], qgot.at[s], q_sem.at[0, s], q_sem.at[1, s], at(0, 1, 0))

    def q_left(s):
        return push(qsend.at[4 + s], qgot.at[4 + s], q_sem.at[0, 4 + s], q_sem.at[1, 4 + s], at(0, 7, 0))

    def q_step(s):
        mine = dq_ref[(z + 4 - s) % 8]
        if s:
            q_right(s - 1).wait_recv()
            mine = mine + qgot[s - 1]
        qsend[s] = mine
        q_right(s).start()
        if s < 3:
            mine = dq_ref[(z + 5 + s) % 8]
            if s:
                q_left(s - 1).wait_recv()
                mine = mine + qgot[4 + s - 1]
            qsend[4 + s] = mine
            q_left(s).start()

    q_step(0)
    for c in load:
        c.wait()

    def add_rows(b, first):
        dh, dl = split(d_all[b])

        def step(t, carry):
            r = pl.ds(pl.multiple_of(t * 256, 256), 256)
            c = ct[b, r, :]
            new = (dot(c, dh) + dot(c, dl)).reshape(2, 2, 64, 256)
            here = pl.ds(t * 2, 2)
            if first:
                acc[here] = new
            else:
                acc[here] = acc[here] + new
            return carry

        lax.fori_loop(0, 8, step, 0)

    add_rows(p, True)
    for i in range(7):
        d_cp[i].wait_recv()
        dy, dx = order[i]
        add_rows(((yl + dy) % 2) * 4 + (x + 4 - dx) % 4, False)
        if i == 2:
            q_step(1)
        if i == 4:
            q_step(2)

    q_step(3)
    c_cp = push(csend, cgot, c_sem.at[0], c_sem.at[1], at(0, 0, 1))
    csend[...] = acc[:, 1 - core]
    c_cp.start()
    c_cp.wait_recv()

    def mine_at(d, a):
        q = a * 8 + (z + d) % 8
        return acc[q, core] + cgot[q]

    def z_right(s, a):
        k = 2 * s + a
        return push(zsend.at[k], zgot.at[k], z_sem.at[0, k], z_sem.at[1, k], at(0, 1, 0))

    def z_left(s, a):
        k = 8 + 2 * s + a
        return push(zsend.at[k], zgot.at[k], z_sem.at[0, k], z_sem.at[1, k], at(0, 7, 0))

    for s in range(4):
        for a in range(2):
            v = mine_at(4 - s, a)
            if s:
                z_right(s - 1, a).wait_recv()
                v = v + zgot[2 * (s - 1) + a]
            zsend[2 * s + a] = v
            z_right(s, a).start()
            if s < 3:
                v = mine_at(5 + s, a)
                if s:
                    z_left(s - 1, a).wait_recv()
                    v = v + zgot[8 + 2 * (s - 1) + a]
                zsend[8 + 2 * s + a] = v
                z_left(s, a).start()

    q_right(3).wait_recv()
    q_left(2).wait_recv()
    d = jnp.transpose(dq_ref[z] + (qgot[3] + qgot[6]))
    qraw = qraw_ref[...]
    inv_norm = lax.rsqrt(jnp.sum(qraw * qraw, axis=1, keepdims=True) + epsilon)
    emb = qraw * inv_norm
    d = inv_norm * (d - emb * jnp.sum(emb * d, axis=1, keepdims=True))
    d = dot3(split(d), split(qo_ref[...]), NT) * gelu_slope(qpre_ref[...])
    qg_ref[...] = dot3(split(d), split(qi_ref[...]), NT)

    inner = split(inner_ref[...])
    own = table_ref[pl.ds(pl.multiple_of(j * 64, 64), 64), :]
    slope = gelu_slope(dot3(split(own), inner))

    for a in range(2):
        z_left(2, a).wait_recv()
        z_right(3, a).wait_recv()
    y_cp = push(ysend, ygot, y_sem.at[0], y_sem.at[1], at(1, 0, 0))

    def block(a):
        return acc[a * 8 + z, core] + cgot[a * 8 + z] + (zgot[6 + a] + zgot[12 + a])

    ysend[...] = block(1 - yh)
    y_cp.start()
    v = block(yh)
    y_cp.wait()
    v = v + ygot[...]
    d = dot3(split(v), split(outer_ref[...]), NT) * slope
    tg_ref[...] = dot3(split(d), inner, NT)

    for c in d_cp:
        c.wait_send()
    c_cp.wait_send()
    for s in range(4):
        q_right(s).wait_send()
        for a in range(2):
            z_right(s, a).wait_send()
    for s in range(3):
        q_left(s).wait_send()
        for a in range(2):
            z_left(s, a).wait_send()


def per_device(
    query_feats,
    item_table,
    serve_ids,
    block_counts,
    item_refs,
    positive,
    query_inner,
    query_outer,
    item_inner,
    item_outer,
):
    lists = serve_ids[0, 0]
    limits = BLOCK * block_counts[0, 0]
    owner = item_refs // CAP
    limit = jnp.zeros_like(item_refs)
    for o in range(8):
        limit = jnp.where(owner == o, limits[o], limit)
    refs = jnp.where(item_refs - owner * CAP < limit, item_refs, -1).T
    pos = jnp.broadcast_to(positive[None, :], (8, 256))

    vm = pl.BlockSpec(memory_space=pltpu.VMEM)
    hbm = pl.BlockSpec(memory_space=pl.ANY)

    def shape(*dims, dtype=f32):
        return jax.ShapeDtypeStruct(dims, dtype)

    def params(number):
        return pltpu.CompilerParams(
            collective_id=number, has_side_effects=True, vmem_limit_bytes=56 << 20
        )

    raw, qpre, qraw, ct, qall, posall = pl.pallas_call(
        pool_kernel,
        name="pool",
        out_shape=[
            shape(256, 256),
            shape(256, 512),
            shape(256, 256),
            shape(8, 2048, 256, dtype=bf16),
            shape(8, 256, 256),
            shape(8, 8, 256, dtype=jnp.int32),
        ],
        in_specs=[vm] * 9,
        out_specs=[vm, vm, vm, hbm, hbm, hbm],
        scratch_shapes=[
            VM((8, 8, 256), jnp.int32),
            VM((256, 2048), bf16),
            VM((256, 2048), bf16),
            VM((512, 256), bf16),
            VM((512, 256), bf16),
            VM((256, 512), bf16),
            VM((256, 512), bf16),
            VM((256, 256), f32),
            VM((8, 2048, 256), bf16),
            VM((7, 256, 256), f32),
            VM((8, 256, 256), f32),
            DMA((2, 7)),
            DMA((2, 7)),
            DMA((2, 7)),
            DMA((2, 7)),
            DMA((8,)),
            DMA((2,)),
        ],
        compiler_params=params(1),
    )(
        refs,
        lists,
        pos,
        item_table,
        item_inner,
        item_outer,
        query_feats,
        query_inner,
        query_outer,
    )

    loss, draw, dq = pl.pallas_call(
        loss_kernel,
        name="loss",
        out_shape=[shape(1, 256), shape(256, 256), shape(8, 256, 256)],
        in_specs=[vm] * 3,
        out_specs=[vm] * 3,
        scratch_shapes=[
            VM((4, 256, 256), f32),
            VM((8, 256, 256), bf16),
            VM((8, 256, 256), bf16),
            VM((4, 256, 256), bf16),
            VM((4, 256, 256), bf16),
            VM((4, 8, 256, 256), f32),
            VM((16, 256), f32),
            VM((8, 16, 256), f32),
            VM((256, 256), f32),
            VM((3, 256, 256), f32),
            VM((3, 256, 256), f32),
            DMA((2, 3)),
            DMA((2, 7)),
            DMA((2, 3)),
        ],
        compiler_params=params(2),
    )(raw, qall, posall)

    query_grad, table_grad = pl.pallas_call(
        table_kernel,
        name="table",
        out_shape=[shape(256, 256), shape(64, 256)],
        in_specs=[vm] * 9 + [hbm],
        out_specs=[vm] * 2,
        scratch_shapes=[
            VM((8, 256, 256), f32),
            VM((8, 2048, 256), bf16),
            VM((16, 2, 64, 256), f32),
            VM((16, 64, 256), f32),
            VM((16, 64, 256), f32),
            VM((14, 64, 256), f32),
            VM((14, 64, 256), f32),
            VM((64, 256), f32),
            VM((64, 256), f32),
            VM((7, 256, 256), f32),
            VM((7, 256, 256), f32),
            DMA((8,)),
            DMA((2, 7)),
            DMA((2,)),
            DMA((2, 14)),
            DMA((2,)),
            DMA((2, 7)),
        ],
        compiler_params=params(3),
    )(draw, dq, qpre, qraw, item_table, item_inner, item_outer, query_inner, query_outer, ct)
    return (loss.reshape(256), query_grad, table_grad)


def solution(mesh):
    placed = (
        P(("pb", "ia"), None),
        P("pb", None),
        P("pb", "ia", None, None),
        P("pb", "ia", None),
        P(("pb", "ia"), None),
        P(("pb", "ia")),
        P(),
        P(),
        P(),
        P(),
    )
    return jax.shard_map(
        per_device,
        mesh=mesh,
        in_specs=placed,
        out_specs=(P(("pb", "ia")), P(("pb", "ia"), None), P(("pb", "ia"), None)),
        check_vma=False,
    )
```

time: 656 us -> 178 us (0.27); the launches traced: 644 us -> 176 us
  waiting for transfers between devices: 345 us -> 0 us
  Pallas kernels: 0 us -> 162 us
  matrix products: 102 us -> 0 us
  blocking collectives: 76.3 us -> 0 us
  other arithmetic: 51.3 us -> 6.99 us
  local copies, waits for them, and re-layouts: 43.7 us -> 5.67 us
  between operations: 14.5 us -> 0.67 us
  starting transfers between devices: 10.8 us -> 0 us
    pallas_call x0 -> x3, Pallas kernels: none -> 162 us  [the longest x1 64.2 us: per_device(): pl.pallas_call(table_kernel, name='table', out_shape=[shape(256, 256), sh...]
    all_gather x2 -> x0, waiting for transfers between devices: 136 us -> none  [the longest x1 121 us: per_device(): block_items = lax.all_gather(item_emb, 'ia', axis=0, tiled=True)]
    reduce_scatter x1 -> x0, waiting for transfers between devices: 110 us -> none  [per_device(): lax.psum_scatter(local_grad, 'ia', scatter_dimension=0, tiled=True)]
    dot_general x12 -> x0, matrix products: 102 us -> none  [the longest x3 49.9 us: matmul_nt(): lax.dot_general(left, right, (((1,), (1,)), ((), ())), precision=highest,...]
    all_to_all x2 -> x0, waiting for transfers between devices: 98.7 us -> none  [the longest x1 49.5 us: per_device(): lax.all_to_all(grad_lists, 'pb', split_axis=0, concat_axis=0, tiled=True)]
    all_gather x2 -> x0, blocking collectives: 76.3 us -> none  [the longest x1 39.6 us: per_device(): lax.all_gather(positive.astype(jnp.float32), 'ia', axis=0, tiled=True)]
    scatter-add x2 -> x0, other arithmetic: 40.8 us -> none  [the longest x1 24.3 us: per_device(): local_grad = jnp.zeros(item_table.shape, jnp.float32).at[row_lists.reshap...]
    gather x4 -> x0, local copies, waits for them, and re-layouts: 33.6 us -> none  [the longest x1 16.1 us: per_device(): outgoing = item_table[row_lists]]
  transfers between devices with their start and end apart: 5 -> 0, of which waited for: 5 -> 0; matrix products, arithmetic and copies ran while one was open for 5% -> 0% of each run, Pallas kernels for 0% -> 0%
where the time goes in v1:
time: 178 us; the launch traced here: 176 us
  Pallas kernels  162 us (91%)
  other arithmetic  6.99 us (4%)
  local copies, waits for them, and re-layouts  5.67 us (3%)
    pallas_call x1, Pallas kernels, per_device(): pl.pallas_call(table_kernel, name='table', out_shape=[shape(256, 256), sh...  64.2 us
    pallas_call x1, Pallas kernels, per_device(): pl.pallas_call(pool_kernel, name='pool', out_shape=[shape(256, 256), shap...  54.7 us
    pallas_call x1, Pallas kernels, per_device(): pl.pallas_call(loss_kernel, name='loss', out_shape=[shape(1, 256), shape(...  43.4 us
    transpose x1, other arithmetic, per_device(): refs = jnp.where(item_refs - owner * CAP < limit, item_refs, -1).T  6.33 us
    unnamed x5, local copies, waits for them, and re-layouts  3.71 us

profile of v1, /device:TPU:1, one launch (start us, length us, event | category | flops | bytes accessed | tf_op | source)
XLA Modules:
  0.0 175.6 jit_solution(5417131979281182107)
XLA Ops:
  0.6 0.7 broadcast_multiply_fusion
  1.3 0.7 fusion.2
  2.0 6.3 %select_bitcast_fusion.refs_ref = s32[8,256]{1,0:T(8,128)} fusion(s32[256,8]{0,1:T(8,128)} %param.14, s32[]{:T(128)} %bitcast.7, s32[]{:T(128)} %bitcast.6, s32[]{:T(128)} %bitcast.5, s32[]{:T(128)} %bitcast.4, s32[]{:T(128)} %bitcast.3, s32[]{:T(128)} %bitcast.2, s32[]{:T(128)} %bitcast.1, s32[]{:T(128)} %bitcast), kind=kLoop, calls=%fused_computation.5 | loop fusion | flops 71680 | bytes 16416 | tf_op jit(solution)/shard_map/transpose | solution.py:574
  8.3 1.3 broadcast_in_dim.41.pos_ref
  9.6 54.7 %pool.1 = (f32[256,256]{1,0:T(8,128)}, f32[256,512]{1,0:T(8,128)}, f32[256,256]{1,0:T(8,128)}, bf16[8,2048,256]{2,1,0:T(8,128)(2,1)}, f32[8,256,256]{2,1,0:T(8,128)}, /*index=5*/s32[8,8,256]{2,1,0:T(8,128)}) custom-call(s32[8,256]{1,0:T(8,128)} %select_bitcast_fusion.refs_ref, s32[8,512]{1,0:T(8,128)} %bitcast.12, s32[8,256]{1,0:T(8,128)} %broadcast_in_dim.41.pos_ref, ...), custom_call_target="tpu_custom_call" | custom-call | tf_op jit(solution)/shard_map/pool/pallas_call | solution.py:588
  64.3 43.4 %loss.1 = (f32[1,256]{1,0:T(1,128)}, f32[256,256]{1,0:T(8,128)}, f32[8,256,256]{2,1,0:T(8,128)}) custom-call(f32[256,256]{1,0:T(8,128)} %get-tuple-element.14.raw_ref, f32[8,256,256]{2,1,0:T(8,128)} %get-tuple-element.15.q_ref, s32[8,8,256]{2,1,0:T(8,128)} %get-tuple-element.16.pos_ref), custom_call_target="tpu_custom_call" | custom-call | tf_op jit(solution)/shard_map/loss/pallas_call | solution.py:633
  107.7 0.0 copy-start
  107.7 64.2 %table.1 = (f32[256,256]{1,0:T(8,128)}, f32[64,256]{1,0:T(8,128)}) custom-call(f32[256,256]{1,0:T(8,128)} %get-tuple-element.18.draw_ref, f32[8,256,256]{2,1,0:T(8,128)} %get-tuple-element.19.dq_ref, f32[256,512]{1,0:T(8,128)} %get-tuple-element.20.qpre_ref, f32[256,256]{1,0:T(8,128)} %get-tuple-element.21.qraw_ref, f32[2048,256]{1,0:T(8,128)} %table_ref.3, ...), custom_call_target="tpu_custom_call" | custom-call | tf_op jit(solution)/shard_map/table/pallas_call | solution.py:658
  171.9 0.0 copy-done
  171.9 0.6 copy.16
  172.5 1.7 copy.17
  174.1 1.5 copy.18
Async XLA Ops:
  107.7 64.2 %copy-start = (f32[1,256]{1,0:T(1,128)S(1)}, f32[1,256]{1,0:T(1,128)}, u32[]{:S(2)}) copy-start(f32[1,256]{1,0:T(1,128)} %get-tuple-element.17) | copy-start | bytes 3076

commit v2 on v0

v2 whole, which is shorter than its diff:
```python
import jax
import jax.numpy as jnp
from jax import lax
from jax.experimental import pallas as pl
from jax.experimental.pallas import tpu as pltpu
from jax.sharding import PartitionSpec as P

BLOCK = 128
CAP = 512
MESH = pl.DeviceIdType.MESH
VM = pltpu.VMEM
DMA = pltpu.SemaphoreType.DMA
f32 = jnp.float32
bf16 = jnp.bfloat16

inverse_temp = 20.0
epsilon = 1e-06

NN = (((1,), (0,)), ((), ()))
NT = (((1,), (1,)), ((), ()))


def split(v):
    hi = v.astype(bf16)
    return hi, (v - hi.astype(f32)).astype(bf16)


def dot(a, b, dims=NN):
    return lax.dot_general(a, b, dims, preferred_element_type=f32)


def lhs(v):
    h, l = split(v)
    return jnp.concatenate([h, h, l], axis=1)


def rhs(v, axis):
    h, l = split(v)
    return jnp.concatenate([h, l, h], axis=axis)


def dot3(a, b, dims=NN):
    return dot(lhs(a), rhs(b, dims[0][1][0]), dims)


def normal_cdf(v):
    return 0.5 * (1.0 + lax.erf(v * 0.7071067811865476))


def gelu(v):
    return v * normal_cdf(v)


def gelu_slope(v):
    return normal_cdf(v) + v * (0.3989422804014327 * jnp.exp(-0.5 * v * v))


def place():
    p, j = lax.axis_index("pb"), lax.axis_index("ia")
    return p, j, p % 4, p // 4, j // 16, (j // 2) % 8, j % 2


def greet(peers):
    barrier = pltpu.get_barrier_semaphore()
    for peer in peers:
        pl.semaphore_signal(barrier, inc=1, device_id=peer, device_id_type=MESH)
    pl.semaphore_wait(barrier, len(peers))


def push(src, dst, sems, k, peer):
    return pltpu.make_async_remote_copy(
        src_ref=src,
        dst_ref=dst,
        send_sem=sems.at[0, k],
        recv_sem=sems.at[1, k],
        device_id=peer,
        device_id_type=MESH,
    )


def step_kernel(
    refs_ref,
    counts_ref,
    lists_ref,
    pos_ref,
    table_ref,
    inner_ref,
    outer_ref,
    qf_ref,
    qi_ref,
    qo_ref,
    loss_ref,
    qg_ref,
    tg_ref,
    live,
    refs_all,
    posb,
    pos_all,
    zcat,
    inncat,
    outcat,
    qall,
    qpre_s,
    qraw_s,
    ct,
    part,
    got,
    items,
    qn,
    qr,
    tcat,
    ex,
    stats,
    stats_all,
    dsend,
    dgot,
    draw,
    d_all,
    dq,
    acc,
    cgot,
    zsend,
    zgot,
    ysend,
    ygot,
    qsend,
    qgot,
    refs_sem,
    pos_sem,
    ring_sem,
    part_sem,
    item_sem,
    stat_sem,
    near_sem,
    d_sem,
    c_sem,
    z_sem,
    y_sem,
    q_sem,
):
    p, j, x, yl, yh, z, core = place()

    def at(dyh, dz, dc):
        return (p, (((yh + dyh) % 2) * 8 + (z + dz) % 8) * 2 + (core + dc) % 2)

    def pbdev(dy, dx):
        return (((yl + dy) % 2) * 4 + (x + dx) % 4, j)

    order = [(1, 0), (0, 1), (0, 3), (0, 2), (1, 1), (1, 3), (1, 2)]
    pb_from = [((yl + dy) % 2) * 4 + (x + 4 - dx) % 4 for dy, dx in order]
    near = [(0, 1), (1, 0), (1, 1)]
    greet(
        [pbdev(*d) for d in order]
        + [at(0, d, 0) for d in range(1, 8)]
        + [at(0, 0, 1), at(1, 0, 0)]
    )

    refs = refs_ref[...]
    owner = refs // CAP
    limit = jnp.zeros((8, 256), jnp.int32)
    for o in range(8):
        limit = jnp.where(owner == o, BLOCK * counts_ref[o], limit)
    live[...] = jnp.where(refs - owner * CAP < limit, refs, -1)
    refs_all[p] = live[...]
    posb[...] = jnp.broadcast_to(pos_ref[...], (8, 256))
    pos_all[z] = posb[...]
    refs_cp = [push(live, refs_all.at[p], refs_sem, i, pbdev(*d)) for i, d in enumerate(order)]
    pos_cp = [push(posb, pos_all.at[z], pos_sem, i, at(0, i + 1, 0)) for i in range(7)]
    for c in refs_cp + pos_cp:
        c.start()

    qpre = dot3(qf_ref[...], qi_ref[...])
    qpre_s[...] = qpre
    qraw = dot3(gelu(qpre), qo_ref[...])
    qraw_s[...] = qraw
    qall[z] = qraw * lax.rsqrt(jnp.sum(qraw * qraw, axis=1, keepdims=True) + epsilon)

    def right(s):
        b = (z + 8 - s) % 8
        return push(qall.at[b], qall.at[b], ring_sem, s, at(0, 1, 0))

    def left(s):
        b = (z + s) % 8
        return push(qall.at[b], qall.at[b], ring_sem, 4 + s, at(0, 7, 0))

    def ring(s):
        if s:
            right(s - 1).wait_recv()
            if s < 4:
                left(s - 1).wait_recv()
        right(s).start()
        if s < 3:
            left(s).start()

    ring(0)

    inncat[...] = lhs(jnp.transpose(inner_ref[...]))
    outcat[...] = lhs(jnp.transpose(outer_ref[...]))

    def rows(t, carry):
        r = pl.ds(pl.multiple_of(t * 256, 256), 256)
        hid = dot(inncat[...], rhs(table_ref[r, :], 1), NT)
        h, l = split(dot(outcat[...], rhs(gelu(hid), 0)))
        zcat[0:256, r] = h
        zcat[256:512, r] = l
        return carry

    lax.fori_loop(0, 8, rows, 0, unroll=2)
    ring(1)

    for c in refs_cp:
        c.wait_recv()

    def piece(s):
        k = s // 2
        dx = (1 - k // 2) * (2 + k) + (k // 2) * (3 - k)
        dy = 1 - s % 2
        return pbdev(dy, dx)

    def part_cp(s):
        return push(part.at[s], got.at[p], part_sem, s, piece(s))

    def pieces(s, carry):
        b = piece(s)[0]
        refs = refs_all[b]
        slot = lax.broadcasted_iota(jnp.int32, (CAP, 256), 0) + p * CAP
        uses = jnp.zeros((CAP, 256), f32)
        for k in range(8):
            uses = uses + jnp.where(slot == refs[k : k + 1, :], 1.0, 0.0)
        uses = uses.astype(bf16)
        listed = lists_ref[pl.ds(b, 1), :]
        for t in range(2):
            row = lax.broadcasted_iota(jnp.int32, (1024, CAP), 0) + t * 1024
            pick = jnp.where(row == listed, 1.0, 0.0).astype(bf16)
            ct[b, t * 1024 : (t + 1) * 1024, :] = dot(pick, uses).astype(bf16)
        total = dot(zcat[...], ct[b])
        total = total[0:256] + total[256:512]

        @pl.when(s < 7)
        def _():
            part[s] = total
            part_cp(s).start()

        @pl.when(s == 7)
        def _():
            got[p] = total

        return carry

    lax.fori_loop(0, 4, pieces, 0)
    ring(2)
    lax.fori_loop(4, 8, pieces, 0)
    ring(3)
    right(3).wait_recv()

    def queries(b, carry):
        q = qall[b]
        qn[b] = rhs(q, 1)
        qr[b] = rhs(q, 0)
        return carry

    lax.fori_loop(0, 8, queries, 0)
    for s in range(7):
        part_cp(s).wait_recv()
    raw = got[0]
    for b in range(1, 8):
        raw = raw + got[b]
    raw = jnp.transpose(raw)
    inv_norm = lax.rsqrt(jnp.sum(raw * raw, axis=1, keepdims=True) + epsilon)
    items[0] = raw * inv_norm

    item_cp = [
        push(items.at[0], items.at[2], item_sem, 1, at(1, 0, 0)),
        push(items.at[0], items.at[1], item_sem, 0, at(0, 0, 1)),
        push(items.at[2], items.at[3], item_sem, 2, at(0, 0, 1)),
    ]
    item_cp[0].start()
    item_cp[1].start()
    stats[...] = jnp.zeros((16, 256), f32)

    def numbers(i):
        row = lax.broadcasted_iota(jnp.int32, (512, 256), 0)
        a = ((yh + i) % 2) * 16 + z * 2
        first, second = (a + core) * 256, (a + 1 - core) * 256 - 256
        return row + jnp.where(row < 256, first, second)

    def logits(i):
        here = lhs(items[2 * i : 2 * i + 2].reshape(512, 256))
        number = numbers(i)

        def step(b, carry):
            lg = inverse_temp * dot(here, qn[b], NT)
            e = jnp.exp(lg)
            ex[i, b] = e
            r = pl.ds(b, 1)
            stats[r, :] = stats[r, :] + jnp.sum(e, axis=0, keepdims=True)
            hit = pos_all[b][0:1, :] == number
            r8 = pl.ds(b + 8, 1)
            stats[r8, :] = stats[r8, :] + jnp.sum(jnp.where(hit, lg, 0.0), axis=0, keepdims=True)
            return carry

        lax.fori_loop(0, 8, step, 0)

    for c in pos_cp:
        c.wait_recv()
    item_cp[1].wait_recv()
    logits(0)
    item_cp[0].wait_recv()
    item_cp[2].start()
    item_cp[2].wait_recv()
    logits(1)

    stat_cp = [push(stats, stats_all.at[z], stat_sem, i, at(0, i + 1, 0)) for i in range(7)]
    for c in stat_cp:
        c.start()
    stats_all[z] = stats[...]
    for i in range(2):
        h, l = split(jnp.transpose(items[2 * i : 2 * i + 2].reshape(512, 256)))
        tcat[i] = jnp.concatenate([h, l, h], axis=1)
    for c in stat_cp:
        c.wait()
    both = stats_all[0]
    for b in range(1, 8):
        both = both + stats_all[b]
    stats[...] = both
    loss_ref[...] = jnp.log(stats[pl.ds(z, 1), :]) - stats[pl.ds(z + 8, 1), :]
    stats[0:8, :] = inverse_temp / both[0:8, :]

    def coefficients(i, b):
        hit = pos_all[b][0:1, :] == numbers(i)
        return split(ex[i, b] * stats[pl.ds(b, 1), :] - jnp.where(hit, inverse_temp, 0.0))

    def item_part(c, b):
        return dot(jnp.concatenate([c[0], c[0], c[1]], axis=1), qr[b])

    def far_items(b, total):
        return total + item_part(coefficients(1, b), b)

    total = lax.fori_loop(0, 8, far_items, jnp.zeros((512, 256), f32))
    to_sib = [push(dsend.at[i], dgot.at[i], near_sem, i, at(0, 0, 1)) for i in range(2)]
    across = push(dsend.at[2], dgot.at[2], near_sem, 2, at(1, 0, 0))
    dsend[0] = total[256:512]
    to_sib[0].start()
    dsend[2] = total[0:256]

    def both_sides(b, total):
        c0, c1 = coefficients(0, b), coefficients(1, b)
        dq[b] = dot(tcat[0], jnp.concatenate([c0[0], c0[0], c0[1]], axis=0)) + dot(
            tcat[1], jnp.concatenate([c1[0], c1[0], c1[1]], axis=0)
        )
        return total + item_part(c0, b)

    def blocks(s, total):
        return both_sides((z + 5 + s) % 8, both_sides((z + 4 - s) % 8, total))

    def q_right(s):
        return push(qsend.at[s], qgot.at[s], q_sem, s, at(0, 1, 0))

    def q_left(s):
        return push(qsend.at[4 + s], qgot.at[4 + s], q_sem, 4 + s, at(0, 7, 0))

    def q_step(s):
        mine = dq[(z + 4 - s) % 8]
        if s:
            q_right(s - 1).wait_recv()
            mine = mine + qgot[s - 1]
        qsend[s] = mine
        q_right(s).start()
        if s < 3:
            mine = dq[(z + 5 + s) % 8]
            if s:
                q_left(s - 1).wait_recv()
                mine = mine + qgot[4 + s - 1]
            qsend[4 + s] = mine
            q_left(s).start()

    total = blocks(0, jnp.zeros((512, 256), f32))
    to_sib[0].wait_recv()
    dsend[2] = dsend[2] + dgot[0]
    across.start()
    q_step(0)
    total = lax.fori_loop(1, 4, blocks, total)
    dsend[1] = total[256:512]
    to_sib[1].start()
    q_step(1)
    to_sib[1].wait_recv()
    mine = total[0:256] + dgot[1]
    across.wait_recv()
    d = mine + dgot[2]
    emb = items[0]
    d = inv_norm * (d - emb * jnp.sum(emb * d, axis=1, keepdims=True))

    for h in range(2):
        draw[h] = d[:, h * 128 : (h + 1) * 128]
        d_all[h, p] = d[:, h * 128 : (h + 1) * 128]

    def d_cp(h, i):
        return push(draw.at[h], d_all.at[h, p], d_sem, h * 7 + i, pbdev(*order[i]))

    for h in range(2):
        for i in range(7):
            d_cp(h, i).start()

    def add_rows(h, b, first):
        dcat = jnp.concatenate(split(d_all[h, b]), axis=1)
        for a in range(2):
            r = dot(ct[b, a * 1024 : (a + 1) * 1024, :], dcat)
            r = (r[:, 0:128] + r[:, 128:256]).reshape(8, 2, 64, 128)
            acc[h, a] = r if first else acc[h, a] + r

    def c_cp(h):
        return push(acc.at[h, :, :, 1 - core], cgot.at[h], c_sem, h, at(0, 0, 1))

    def z_right(h, s):
        return push(zsend.at[h, s], zgot.at[h, s], z_sem, h * 7 + s, at(0, 1, 0))

    def z_left(h, s):
        return push(zsend.at[h, 4 + s], zgot.at[h, 4 + s], z_sem, h * 7 + 4 + s, at(0, 7, 0))

    def rows_of(h, d):
        return acc[h, :, (z + d) % 8, core] + cgot[h, :, (z + d) % 8]

    def z_step(h, s):
        v = rows_of(h, 4 - s)
        if s:
            z_right(h, s - 1).wait_recv()
            v = v + zgot[h, s - 1]
        zsend[h, s] = v
        z_right(h, s).start()
        if s < 3:
            v = rows_of(h, 5 + s)
            if s:
                z_left(h, s - 1).wait_recv()
                v = v + zgot[h, 4 + s - 1]
            zsend[h, 4 + s] = v
            z_left(h, s).start()

    add_rows(0, p, True)
    add_rows(1, p, True)
    for i in range(7):
        if i == 3:
            q_step(2)
        d_cp(0, i).wait_recv()
        add_rows(0, pb_from[i], False)
    c_cp(0).start()
    q_step(3)
    c_cp(0).wait_recv()
    z_step(0, 0)
    for i in range(7):
        d_cp(1, i).wait_recv()
        add_rows(1, pb_from[i], False)
        if i in (1, 3, 5):
            z_step(0, (i + 1) // 2)
    c_cp(1).start()

    y_cp = [push(ysend.at[h], ygot.at[h], y_sem, h, at(1, 0, 0)) for h in range(2)]

    def to_y(h):
        z_left(h, 2).wait_recv()
        z_right(h, 3).wait_recv()
        v = rows_of(h, 0) + (zgot[h, 3] + zgot[h, 6])
        zgot[h, 0] = v
        ysend[h] = zgot[h, 0, 1 - yh]
        y_cp[h].start()

    c_cp(1).wait_recv()
    z_step(1, 0)
    to_y(0)
    q_right(3).wait_recv()
    q_left(2).wait_recv()
    d = jnp.transpose(dq[z] + (qgot[3] + qgot[6]))
    qraw = qraw_s[...]
    inv_norm = lax.rsqrt(jnp.sum(qraw * qraw, axis=1, keepdims=True) + epsilon)
    emb = qraw * inv_norm
    d = inv_norm * (d - emb * jnp.sum(emb * d, axis=1, keepdims=True))
    d = dot3(d, qo_ref[...], NT) * gelu_slope(qpre_s[...])
    z_step(1, 1)
    qg_ref[...] = dot3(d, qi_ref[...], NT)
    z_step(1, 2)
    own = table_ref[pl.ds(pl.multiple_of(j * 64, 64), 64), :]
    slope = gelu_slope(dot3(own, inner_ref[...]))
    z_step(1, 3)
    to_y(1)
    y_cp[0].wait_recv()
    y_cp[1].wait_recv()
    v = jnp.concatenate([zgot[h, 0, yh] + ygot[h] for h in range(2)], axis=1)
    d = dot3(v, outer_ref[...], NT) * slope
    tg_ref[...] = dot3(d, inner_ref[...], NT)

    for c in refs_cp + pos_cp + item_cp + to_sib + [across] + y_cp:
        c.wait_send()
    for s in range(4):
        right(s).wait_send()
        q_right(s).wait_send()
    for s in range(3):
        left(s).wait_send()
        q_left(s).wait_send()
    for s in range(7):
        part_cp(s).wait_send()
    for h in range(2):
        c_cp(h).wait_send()
        for i in range(7):
            d_cp(h, i).wait_send()
        for s in range(4):
            z_right(h, s).wait_send()
        for s in range(3):
            z_left(h, s).wait_send()


def per_device(
    query_feats,
    item_table,
    serve_ids,
    block_counts,
    item_refs,
    positive,
    query_inner,
    query_outer,
    item_inner,
    item_outer,
):
    vm = pl.BlockSpec(memory_space=pltpu.VMEM)
    sm = pl.BlockSpec(memory_space=pltpu.SMEM)
    loss, query_grad, table_grad = pl.pallas_call(
        step_kernel,
        name="step",
        out_shape=[
            jax.ShapeDtypeStruct((1, 256), f32),
            jax.ShapeDtypeStruct((256, 256), f32),
            jax.ShapeDtypeStruct((64, 256), f32),
        ],
        in_specs=[vm, sm] + [vm] * 8,
        out_specs=[vm] * 3,
        scratch_shapes=[
            VM((8, 256), jnp.int32),
            VM((8, 8, 256), jnp.int32),
            VM((8, 256), jnp.int32),
            VM((8, 8, 256), jnp.int32),
            VM((512, 2048), bf16),
            VM((512, 768), bf16),
            VM((256, 1536), bf16),
            VM((8, 256, 256), f32),
            VM((256, 512), f32),
            VM((256, 256), f32),
            VM((8, 2048, 256), bf16),
            VM((7, 256, 256), f32),
            VM((8, 256, 256), f32),
            VM((4, 256, 256), f32),
            VM((8, 256, 768), bf16),
            VM((8, 768, 256), bf16),
            VM((2, 256, 1536), bf16),
            VM((2, 8, 512, 256), f32),
            VM((16, 256), f32),
            VM((8, 16, 256), f32),
            VM((3, 256, 256), f32),
            VM((3, 256, 256), f32),
            VM((2, 256, 128), f32),
            VM((2, 8, 256, 128), f32),
            VM((8, 256, 256), f32),
            VM((2, 2, 8, 2, 64, 128), f32),
            VM((2, 2, 8, 64, 128), f32),
            VM((2, 7, 2, 64, 128), f32),
            VM((2, 7, 2, 64, 128), f32),
            VM((2, 64, 128), f32),
            VM((2, 64, 128), f32),
            VM((7, 256, 256), f32),
            VM((7, 256, 256), f32),
            DMA((2, 7)),
            DMA((2, 7)),
            DMA((2, 7)),
            DMA((2, 7)),
            DMA((2, 3)),
            DMA((2, 7)),
            DMA((2, 3)),
            DMA((2, 14)),
            DMA((2, 2)),
            DMA((2, 14)),
            DMA((2, 2)),
            DMA((2, 7)),
        ],
        compiler_params=pltpu.CompilerParams(
            collective_id=1, has_side_effects=True, vmem_limit_bytes=60 << 20
        ),
    )(
        item_refs.T,
        block_counts[0, 0],
        serve_ids[0, 0],
        positive.reshape(1, 256),
        item_table,
        item_inner,
        item_outer,
        query_feats,
        query_inner,
        query_outer,
    )
    return (loss.reshape(256), query_grad, table_grad)


def solution(mesh):
    placed = (
        P(("pb", "ia"), None),
        P("pb", None),
        P("pb", "ia", None, None),
        P("pb", "ia", None),
        P(("pb", "ia"), None),
        P(("pb", "ia")),
        P(),
        P(),
        P(),
        P(),
    )
    return jax.shard_map(
        per_device,
        mesh=mesh,
        in_specs=placed,
        out_specs=(P(("pb", "ia")), P(("pb", "ia"), None), P(("pb", "ia"), None)),
        check_vma=False,
    )
```

time: 656 us -> 146 us (0.22)
  the two profiles are of different devices: /device:TPU:1 before, /device:TPU:14 now
where the time goes in v2:
time: 146 us; the launch traced here: 145 us
  Pallas kernels  140 us (96%)
  local copies, waits for them, and re-layouts  4.38 us (3%)
    pallas_call x1, Pallas kernels, per_device(): pl.pallas_call(step_kernel, name='step', out_shape=[jax.ShapeDtypeStruct(...  140 us
    unnamed x3, local copies, waits for them, and re-layouts  4.38 us

profile of v2, /device:TPU:14, one launch (start us, length us, event | category | flops | bytes accessed | tf_op | source)
XLA Modules:
  0.0 145.5 jit_solution(18107959941916696200)
XLA Ops:
  0.6 140.5 %step.1 = (f32[1,256]{1,0:T(1,128)}, f32[256,256]{1,0:T(8,128)}, f32[64,256]{1,0:T(8,128)}) custom-call(s32[8,256]{1,0:T(8,128)} %bitcast.6, s32[8]{0:T(128)} %bitcast.9, s32[8,512]{1,0:T(8,128)} %bitcast.5, s32[1,256]{1,0:T(1,128)} %bitcast.8, f32[2048,256]{1,0:T(8,128)} %table_ref.1, f32[256,512]{1,0:T(8,128)} %inner_ref.1, f32[512,256]{1,0:T(8,128)} %outer_ref.1, ...), custom_call_target="tpu_custom_call" | custom-call | tf_op jit(solution)/shard_map/step/pallas_call | solution.py:524
  141.1 1.2 copy.16
  142.4 1.7 %copy.17 = f32[256,256]{1,0:T(8,128)} copy(f32[256,256]{1,0:T(8,128)} %get-tuple-element.13) | data formatting | bytes 524288
  144.0 1.5 %copy.18 = f32[64,256]{1,0:T(8,128)} copy(f32[64,256]{1,0:T(8,128)} %get-tuple-element.14) | data formatting | bytes 131072

commit v3 on v2

--- a/solution.py
+++ b/solution.py
@@ -83,15 +83,21 @@
     counts_ref,
     lists_ref,
     pos_ref,
+    table_hbm,
+    inner_hbm,
+    outer_hbm,
+    qf_hbm,
+    qi_hbm,
+    qo_hbm,
+    loss_ref,
+    qg_ref,
+    tg_ref,
     table_ref,
     inner_ref,
     outer_ref,
     qf_ref,
     qi_ref,
     qo_ref,
-    loss_ref,
-    qg_ref,
-    tg_ref,
     live,
     refs_all,
     posb,
@@ -119,26 +125,44 @@
     dq,
     acc,
     cgot,
-    zsend,
-    zgot,
-    ysend,
-    ygot,
+    esum,
+    egot,
+    vcat,
+    outr,
+    innr,
+    slope,
     qsend,
     qgot,
+    load_sem,
     refs_sem,
     pos_sem,
     ring_sem,
+    zt_sem,
     part_sem,
     item_sem,
     stat_sem,
     near_sem,
     d_sem,
     c_sem,
-    z_sem,
-    y_sem,
+    e_sem,
     q_sem,
 ):
     p, j, x, yl, yh, z, core = place()
+    loads = [
+        pltpu.make_async_copy(src, dst, load_sem.at[i])
+        for i, (src, dst) in enumerate(
+            [
+                (qf_hbm, qf_ref),
+                (qi_hbm, qi_ref),
+                (qo_hbm, qo_ref),
+                (inner_hbm, inner_ref),
+                (outer_hbm, outer_ref),
+                (table_hbm, table_ref),
+            ]
+        )
+    ]
+    for c in loads:
+        c.start()
 
     def at(dyh, dz, dc):
         return (p, (((yh + dyh) % 2) * 8 + (z + dz) % 8) * 2 + (core + dc) % 2)
@@ -148,11 +172,11 @@
 
     order = [(1, 0), (0, 1), (0, 3), (0, 2), (1, 1), (1, 3), (1, 2)]
     pb_from = [((yl + dy) % 2) * 4 + (x + 4 - dx) % 4 for dy, dx in order]
-    near = [(0, 1), (1, 0), (1, 1)]
+    others = [(a, d) for d in (4, 3, 5, 2, 6, 1, 7, 0) for a in (0, 1) if a or d]
     greet(
         [pbdev(*d) for d in order]
-        + [at(0, d, 0) for d in range(1, 8)]
-        + [at(0, 0, 1), at(1, 0, 0)]
+        + [at(a, d, 0) for a, d in others]
+        + [at(0, 0, 1)]
     )
 
     refs = refs_ref[...]
@@ -169,6 +193,8 @@
     for c in refs_cp + pos_cp:
         c.start()
 
+    for c in loads[:3]:
+        c.wait()
     qpre = dot3(qf_ref[...], qi_ref[...])
     qpre_s[...] = qpre
     qraw = dot3(gelu(qpre), qo_ref[...])
@@ -194,19 +220,37 @@
 
     ring(0)
 
+    for c in loads[3:]:
+        c.wait()
     inncat[...] = lhs(jnp.transpose(inner_ref[...]))
     outcat[...] = lhs(jnp.transpose(outer_ref[...]))
 
-    def rows(t, carry):
+    def share(i):
+        t = core * 4 + i
+        return push(dq.at[t], dq.at[t], zt_sem, i, at(0, 0, 1))
+
+    def keep(t):
+        r = pl.ds(pl.multiple_of(t * 256, 256), 256)
+        h, l = split(dq[t])
+        zcat[0:256, r] = h
+        zcat[256:512, r] = l
+
+    def rows(i, carry):
+        t = core * 4 + i
         r = pl.ds(pl.multiple_of(t * 256, 256), 256)
         hid = dot(inncat[...], rhs(table_ref[r, :], 1), NT)
-        h, l = split(dot(outcat[...], rhs(gelu(hid), 0)))
-        zcat[0:256, r] = h
-        zcat[256:512, r] = l
+        dq[t] = dot(outcat[...], rhs(gelu(hid), 0))
+        share(i).start()
+        keep(t)
         return carry
 
-    lax.fori_loop(0, 8, rows, 0, unroll=2)
+    lax.fori_loop(0, 4, rows, 0, unroll=2)
     ring(1)
+    for i in range(4):
+        share(i).wait_recv()
+        keep((1 - core) * 4 + i)
+    for i in range(4):
+        share(i).wait_send()
 
     for c in refs_cp:
         c.wait_recv()
@@ -284,14 +328,17 @@
         first, second = (a + core) * 256, (a + 1 - core) * 256 - 256
         return row + jnp.where(row < 256, first, second)
 
-    def logits(i):
-        here = lhs(items[2 * i : 2 * i + 2].reshape(512, 256))
-        number = numbers(i)
+    def logits(i, first, last):
+        if last - first == 512:
+            here = lhs(items[2 * i : 2 * i + 2].reshape(512, 256))
+        else:
+            here = lhs(items[2 * i + first // 256])
+        number = numbers(i)[first:last]
 
         def step(b, carry):
             lg = inverse_temp * dot(here, qn[b], NT)
             e = jnp.exp(lg)
-            ex[i, b] = e
+            ex[i, b, first:last] = e
             r = pl.ds(b, 1)
             stats[r, :] = stats[r, :] + jnp.sum(e, axis=0, keepdims=True)
             hit = pos_all[b][0:1, :] == number
@@ -304,11 +351,12 @@
     for c in pos_cp:
         c.wait_recv()
     item_cp[1].wait_recv()
-    logits(0)
+    logits(0, 0, 512)
     item_cp[0].wait_recv()
     item_cp[2].start()
+    logits(1, 0, 256)
     item_cp[2].wait_recv()
-    logits(1)
+    logits(1, 256, 512)
 
     stat_cp = [push(stats, stats_all.at[z], stat_sem, i, at(0, i + 1, 0)) for i in range(7)]
     for c in stat_cp:
@@ -317,13 +365,18 @@
     for i in range(2):
         h, l = split(jnp.transpose(items[2 * i : 2 * i + 2].reshape(512, 256)))
         tcat[i] = jnp.concatenate([h, l, h], axis=1)
+    outr[...] = rhs(outer_ref[...], 1)
+    innr[...] = rhs(inner_ref[...], 1)
+    own = table_ref[pl.ds(pl.multiple_of(j * 64, 64), 64), :]
+    slope[...] = gelu_slope(dot3(own, inner_ref[...]))
     for c in stat_cp:
         c.wait()
     both = stats_all[0]
     for b in range(1, 8):
         both = both + stats_all[b]
     stats[...] = both
-    loss_ref[...] = jnp.log(stats[pl.ds(z, 1), :]) - stats[pl.ds(z + 8, 1), :]
+    loss = jnp.log(stats[pl.ds(z, 1), :]) - stats[pl.ds(z + 8, 1), :]
+    loss_ref[...] = loss.reshape(256)
     stats[0:8, :] = inverse_temp / both[0:8, :]
 
     def coefficients(i, b):
@@ -333,15 +386,22 @@
     def item_part(c, b):
         return dot(jnp.concatenate([c[0], c[0], c[1]], axis=1), qr[b])
 
-    def far_items(b, total):
-        return total + item_part(coefficients(1, b), b)
-
-    total = lax.fori_loop(0, 8, far_items, jnp.zeros((512, 256), f32))
+    def far_items(first):
+        def step(b, total):
+            hit = pos_all[b][0:1, :] == numbers(1)[first : first + 256]
+            c = ex[1, b, first : first + 256] * stats[pl.ds(b, 1), :]
+            return total + item_part(split(c - jnp.where(hit, inverse_temp, 0.0)), b)
+
+        return lax.fori_loop(0, 8, step, jnp.zeros((256, 256), f32), unroll=2)
+
     to_sib = [push(dsend.at[i], dgot.at[i], near_sem, i, at(0, 0, 1)) for i in range(2)]
     across = push(dsend.at[2], dgot.at[2], near_sem, 2, at(1, 0, 0))
-    dsend[0] = total[256:512]
+    dsend[0] = far_items(256)
     to_sib[0].start()
-    dsend[2] = total[0:256]
+    total = far_items(0)
+    to_sib[0].wait_recv()
+    dsend[2] = total + dgot[0]
+    across.start()
 
     def both_sides(b, total):
         c0, c1 = coefficients(0, b), coefficients(1, b)
@@ -375,9 +435,6 @@
             q_left(s).start()
 
     total = blocks(0, jnp.zeros((512, 256), f32))
-    to_sib[0].wait_recv()
-    dsend[2] = dsend[2] + dgot[0]
-    across.start()
     q_step(0)
     total = lax.fori_loop(1, 4, blocks, total)
     dsend[1] = total[256:512]
@@ -411,61 +468,32 @@
     def c_cp(h):
         return push(acc.at[h, :, :, 1 - core], cgot.at[h], c_sem, h, at(0, 0, 1))
 
-    def z_right(h, s):
-        return push(zsend.at[h, s], zgot.at[h, s], z_sem, h * 7 + s, at(0, 1, 0))
-
-    def z_left(h, s):
-        return push(zsend.at[h, 4 + s], zgot.at[h, 4 + s], z_sem, h * 7 + 4 + s, at(0, 7, 0))
-
-    def rows_of(h, d):
-        return acc[h, :, (z + d) % 8, core] + cgot[h, :, (z + d) % 8]
-
-    def z_step(h, s):
-        v = rows_of(h, 4 - s)
-        if s:
-            z_right(h, s - 1).wait_recv()
-            v = v + zgot[h, s - 1]
-        zsend[h, s] = v
-        z_right(h, s).start()
-        if s < 3:
-            v = rows_of(h, 5 + s)
-            if s:
-                z_left(h, s - 1).wait_recv()
-                v = v + zgot[h, 4 + s - 1]
-            zsend[h, 4 + s] = v
-            z_left(h, s).start()
+    def e_cp(h, k):
+        a, d = others[k]
+        src = esum.at[h, (yh + a) % 2, (z + d) % 8]
+        return push(src, egot.at[h, k], e_sem, h * 15 + k, at(a, d, 0))
+
+    def send_rows(h):
+        c_cp(h).wait_recv()
+        esum[h] = acc[h, :, :, core] + cgot[h]
+        for k in range(15):
+            e_cp(h, k).start()
 
     add_rows(0, p, True)
     add_rows(1, p, True)
     for i in range(7):
-        if i == 3:
+        if i == 2:
             q_step(2)
         d_cp(0, i).wait_recv()
         add_rows(0, pb_from[i], False)
     c_cp(0).start()
     q_step(3)
-    c_cp(0).wait_recv()
-    z_step(0, 0)
+    send_rows(0)
     for i in range(7):
         d_cp(1, i).wait_recv()
         add_rows(1, pb_from[i], False)
-        if i in (1, 3, 5):
-            z_step(0, (i + 1) // 2)
     c_cp(1).start()
-
-    y_cp = [push(ysend.at[h], ygot.at[h], y_sem, h, at(1, 0, 0)) for h in range(2)]
-
-    def to_y(h):
-        z_left(h, 2).wait_recv()
-        z_right(h, 3).wait_recv()
-        v = rows_of(h, 0) + (zgot[h, 3] + zgot[h, 6])
-        zgot[h, 0] = v
-        ysend[h] = zgot[h, 0, 1 - yh]
-        y_cp[h].start()
-
-    c_cp(1).wait_recv()
-    z_step(1, 0)
-    to_y(0)
+    send_rows(1)
     q_right(3).wait_recv()
     q_left(2).wait_recv()
     d = jnp.transpose(dq[z] + (qgot[3] + qgot[6]))
@@ -474,20 +502,18 @@
     emb = qraw * inv_norm
     d = inv_norm * (d - emb * jnp.sum(emb * d, axis=1, keepdims=True))
     d = dot3(d, qo_ref[...], NT) * gelu_slope(qpre_s[...])
-    z_step(1, 1)
     qg_ref[...] = dot3(d, qi_ref[...], NT)
-    z_step(1, 2)
-    own = table_ref[pl.ds(pl.multiple_of(j * 64, 64), 64), :]
-    slope = gelu_slope(dot3(own, inner_ref[...]))
-    z_step(1, 3)
-    to_y(1)
-    y_cp[0].wait_recv()
-    y_cp[1].wait_recv()
-    v = jnp.concatenate([zgot[h, 0, yh] + ygot[h] for h in range(2)], axis=1)
-    d = dot3(v, outer_ref[...], NT) * slope
-    tg_ref[...] = dot3(d, inner_ref[...], NT)
-
-    for c in refs_cp + pos_cp + item_cp + to_sib + [across] + y_cp:
+    for h in range(2):
+        for k in range(15):
+            e_cp(h, k).wait_recv()
+        v = esum[h, yh, z]
+        for k in range(15):
+            v = v + egot[h, k]
+        vcat[:, h * 128 : (h + 1) * 128] = v
+    d = dot(lhs(vcat[...]), outr[...], NT) * slope[...]
+    tg_ref[...] = dot(lhs(d), innr[...], NT)
+
+    for c in refs_cp + pos_cp + item_cp + to_sib + [across]:
         c.wait_send()
     for s in range(4):
         right(s).wait_send()
@@ -501,10 +527,14 @@
         c_cp(h).wait_send()
         for i in range(7):
             d_cp(h, i).wait_send()
-        for s in range(4):
-            z_right(h, s).wait_send()
-        for s in range(3):
-            z_left(h, s).wait_send()
+        for k in range(15):
+            e_cp(h, k).wait_send()
+
+
+def keep_kernel(a_ref, b_ref, c_ref, a_out, b_out, c_out):
+    a_out[...] = a_ref[...]
+    b_out[...] = b_ref[...]
+    c_out[...] = c_ref[...]
 
 
 def per_device(
@@ -521,17 +551,24 @@
 ):
     vm = pl.BlockSpec(memory_space=pltpu.VMEM)
     sm = pl.BlockSpec(memory_space=pltpu.SMEM)
+    hbm = pl.BlockSpec(memory_space=pl.ANY)
     loss, query_grad, table_grad = pl.pallas_call(
         step_kernel,
         name="step",
         out_shape=[
-            jax.ShapeDtypeStruct((1, 256), f32),
+            jax.ShapeDtypeStruct((256,), f32),
             jax.ShapeDtypeStruct((256, 256), f32),
             jax.ShapeDtypeStruct((64, 256), f32),
         ],
-        in_specs=[vm, sm] + [vm] * 8,
+        in_specs=[vm, sm, vm, vm] + [hbm] * 6,
         out_specs=[vm] * 3,
         scratch_shapes=[
+            VM((2048, 256), f32),
+            VM((256, 512), f32),
+            VM((512, 256), f32),
+            VM((256, 256), f32),
+            VM((256, 512), f32),
+            VM((512, 256), f32),
             VM((8, 256), jnp.int32),
             VM((8, 8, 256), jnp.int32),
             VM((8, 256), jnp.int32),
@@ -559,23 +596,26 @@
             VM((8, 256, 256), f32),
             VM((2, 2, 8, 2, 64, 128), f32),
             VM((2, 2, 8, 64, 128), f32),
-            VM((2, 7, 2, 64, 128), f32),
-            VM((2, 7, 2, 64, 128), f32),
-            VM((2, 64, 128), f32),
-            VM((2, 64, 128), f32),
+            VM((2, 2, 8, 64, 128), f32),
+            VM((2, 15, 64, 128), f32),
+            VM((64, 256), f32),
+            VM((512, 768), bf16),
+            VM((256, 1536), bf16),
+            VM((64, 512), f32),
             VM((7, 256, 256), f32),
             VM((7, 256, 256), f32),
+            DMA((6,)),
             DMA((2, 7)),
             DMA((2, 7)),
             DMA((2, 7)),
+            DMA((2, 4)),
             DMA((2, 7)),
             DMA((2, 3)),
             DMA((2, 7)),
             DMA((2, 3)),
             DMA((2, 14)),
             DMA((2, 2)),
-            DMA((2, 14)),
-            DMA((2, 2)),
+            DMA((2, 30)),
             DMA((2, 7)),
         ],
         compiler_params=pltpu.CompilerParams(
@@ -593,7 +633,17 @@
         query_inner,
         query_outer,
     )
-    return (loss.reshape(256), query_grad, table_grad)
+    return pl.pallas_call(
+        keep_kernel,
+        name="keep",
+        out_shape=[
+            jax.ShapeDtypeStruct((256,), f32),
+            jax.ShapeDtypeStruct((256, 256), f32),
+            jax.ShapeDtypeStruct((64, 256), f32),
+        ],
+        in_specs=[vm] * 3,
+        out_specs=[vm] * 3,
+    )(loss, query_grad, table_grad)
 
 
 def solution(mesh):

time: 146 us -> 140 us (0.959)
  the two profiles are of different devices: /device:TPU:14 before, /device:TPU:1 now
where the time goes in v3:
time: 140 us; the launch traced here: 138 us
  Pallas kernels  137 us (98%)
    pallas_call x1, Pallas kernels, per_device(): pl.pallas_call(step_kernel, name='step', out_shape=[jax.ShapeDtypeStruct(...  135 us

profile of v3, /device:TPU:1, one launch (start us, length us, event | category | flops | bytes accessed | tf_op | source)
XLA Modules:
  0.0 137.8 jit_solution(12459615051310247146)
XLA Ops:
  0.6 135.5 %step.1 = (f32[256]{0:T(256)}, f32[256,256]{1,0:T(8,128)}, f32[64,256]{1,0:T(8,128)}) custom-call(s32[8,256]{1,0:T(8,128)} %bitcast.5, s32[8]{0:T(128)} %bitcast.7, s32[8,512]{1,0:T(8,128)} %bitcast.4, s32[1,256]{1,0:T(1,128)} %bitcast.6, f32[2048,256]{1,0:T(8,128)} %table_hbm.1, f32[256,512]{1,0:T(8,128)} %inner_hbm.1, f32[512,256]{1,0:T(8,128)} %outer_hbm.1, ...), custom_call_target="tpu_custom_call" | custom-call | tf_op jit(solution)/shard_map/step/pallas_call | solution.py:555
  136.1 1.7 %keep.1 = (f32[256]{0:T(256)}, f32[256,256]{1,0:T(8,128)}, f32[64,256]{1,0:T(8,128)}) custom-call(f32[256]{0:T(256)} %get-tuple-element.6.a_ref, f32[256,256]{1,0:T(8,128)} %get-tuple-element.7.b_ref, f32[64,256]{1,0:T(8,128)} %get-tuple-element.8.c_ref), custom_call_target="tpu_custom_call" | custom-call | tf_op jit(solution)/shard_map/keep/pallas_call | solution.py:636

commit v4 on v3

--- a/solution.py
+++ b/solution.py
@@ -413,26 +413,30 @@
     def blocks(s, total):
         return both_sides((z + 5 + s) % 8, both_sides((z + 4 - s) % 8, total))
 
-    def q_right(s):
-        return push(qsend.at[s], qgot.at[s], q_sem, s, at(0, 1, 0))
-
-    def q_left(s):
-        return push(qsend.at[4 + s], qgot.at[4 + s], q_sem, 4 + s, at(0, 7, 0))
+    def q_right(s, u):
+        r = pl.ds(128 * u, 128)
+        return push(qsend.at[s, r], qgot.at[s, r], q_sem, 2 * s + u, at(0, 1, 0))
+
+    def q_left(s, u):
+        r = pl.ds(128 * u, 128)
+        return push(qsend.at[4 + s, r], qgot.at[4 + s, r], q_sem, 8 + 2 * s + u, at(0, 7, 0))
 
     def q_step(s):
-        mine = dq[(z + 4 - s) % 8]
-        if s:
-            q_right(s - 1).wait_recv()
-            mine = mine + qgot[s - 1]
-        qsend[s] = mine
-        q_right(s).start()
-        if s < 3:
-            mine = dq[(z + 5 + s) % 8]
+        for u in range(2):
+            r = slice(128 * u, 128 * u + 128)
+            mine = dq[(z + 4 - s) % 8, r]
             if s:
-                q_left(s - 1).wait_recv()
-                mine = mine + qgot[4 + s - 1]
-            qsend[4 + s] = mine
-            q_left(s).start()
+                q_right(s - 1, u).wait_recv()
+                mine = mine + qgot[s - 1, r]
+            qsend[s, r] = mine
+            q_right(s, u).start()
+            if s < 3:
+                mine = dq[(z + 5 + s) % 8, r]
+                if s:
+                    q_left(s - 1, u).wait_recv()
+                    mine = mine + qgot[4 + s - 1, r]
+                qsend[4 + s, r] = mine
+                q_left(s, u).start()
 
     total = blocks(0, jnp.zeros((512, 256), f32))
     q_step(0)
@@ -482,20 +486,22 @@
     add_rows(0, p, True)
     add_rows(1, p, True)
     for i in range(7):
+        if i == 0:
+            q_step(2)
         if i == 2:
-            q_step(2)
+            q_step(3)
         d_cp(0, i).wait_recv()
         add_rows(0, pb_from[i], False)
     c_cp(0).start()
-    q_step(3)
     send_rows(0)
     for i in range(7):
         d_cp(1, i).wait_recv()
         add_rows(1, pb_from[i], False)
     c_cp(1).start()
     send_rows(1)
-    q_right(3).wait_recv()
-    q_left(2).wait_recv()
+    for u in range(2):
+        q_right(3, u).wait_recv()
+        q_left(2, u).wait_recv()
     d = jnp.transpose(dq[z] + (qgot[3] + qgot[6]))
     qraw = qraw_s[...]
     inv_norm = lax.rsqrt(jnp.sum(qraw * qraw, axis=1, keepdims=True) + epsilon)
@@ -517,10 +523,12 @@
         c.wait_send()
     for s in range(4):
         right(s).wait_send()
-        q_right(s).wait_send()
+        q_right(s, 0).wait_send()
+        q_right(s, 1).wait_send()
     for s in range(3):
         left(s).wait_send()
-        q_left(s).wait_send()
+        q_left(s, 0).wait_send()
+        q_left(s, 1).wait_send()
     for s in range(7):
         part_cp(s).wait_send()
     for h in range(2):
@@ -616,7 +624,7 @@
             DMA((2, 14)),
             DMA((2, 2)),
             DMA((2, 30)),
-            DMA((2, 7)),
+            DMA((2, 14)),
         ],
         compiler_params=pltpu.CompilerParams(
             collective_id=1, has_side_effects=True, vmem_limit_bytes=60 << 20

time: 140 us -> 137 us (0.979); the launches traced: 138 us -> 137 us
  no operation moved by 1% of the time
where the time goes in v4:
time: 137 us
  Pallas kernels  136 us (99%)
    pallas_call x1, Pallas kernels, per_device(): pl.pallas_call(step_kernel, name='step', out_shape=[jax.ShapeDtypeStruct(...  134 us

profile of v4, /device:TPU:1, one launch (start us, length us, event | category | flops | bytes accessed | tf_op | source)
XLA Modules:
  0.0 136.5 jit_solution(6892540655556323760)
XLA Ops:
  0.6 134.2 %step.1 = (f32[256]{0:T(256)}, f32[256,256]{1,0:T(8,128)}, f32[64,256]{1,0:T(8,128)}) custom-call(s32[8,256]{1,0:T(8,128)} %bitcast.5, s32[8]{0:T(128)} %bitcast.7, s32[8,512]{1,0:T(8,128)} %bitcast.4, s32[1,256]{1,0:T(1,128)} %bitcast.6, f32[2048,256]{1,0:T(8,128)} %table_hbm.1, f32[256,512]{1,0:T(8,128)} %inner_hbm.1, f32[512,256]{1,0:T(8,128)} %outer_hbm.1, ...), custom_call_target="tpu_custom_call" | custom-call | tf_op jit(solution)/shard_map/step/pallas_call | solution.py:563
  134.9 1.7 %keep.1 = (f32[256]{0:T(256)}, f32[256,256]{1,0:T(8,128)}, f32[64,256]{1,0:T(8,128)}) custom-call(f32[256]{0:T(256)} %get-tuple-element.6.a_ref, f32[256,256]{1,0:T(8,128)} %get-tuple-element.7.b_ref, f32[64,256]{1,0:T(8,128)} %get-tuple-element.8.c_ref), custom_call_target="tpu_custom_call" | custom-call | tf_op jit(solution)/shard_map/keep/pallas_call | solution.py:644

commit v5 on v4

--- a/solution.py
+++ b/solution.py
@@ -304,11 +304,11 @@
         return carry
 
     lax.fori_loop(0, 8, queries, 0)
+    raw = got[p]
     for s in range(7):
         part_cp(s).wait_recv()
-    raw = got[0]
-    for b in range(1, 8):
-        raw = raw + got[b]
+        dx = (2, 3, 1, 0)[s // 2]
+        raw = raw + got[((yl + 1 - s % 2) % 2) * 4 + (x + 4 - dx) % 4]
     raw = jnp.transpose(raw)
     inv_norm = lax.rsqrt(jnp.sum(raw * raw, axis=1, keepdims=True) + epsilon)
     items[0] = raw * inv_norm
@@ -358,7 +358,12 @@
     item_cp[2].wait_recv()
     logits(1, 256, 512)
 
-    stat_cp = [push(stats, stats_all.at[z], stat_sem, i, at(0, i + 1, 0)) for i in range(7)]
+    upper, lower = pl.ds(0, 8), pl.ds(8, 8)
+    stat_cp = [
+        push(stats.at[r], stats_all.at[z, r], stat_sem, 7 * k + i, at(0, i + 1, 0))
+        for k, r in enumerate((upper, lower))
+        for i in (3, 2, 4, 1, 5, 0, 6)
+    ]
     for c in stat_cp:
         c.start()
     stats_all[z] = stats[...]
@@ -369,15 +374,13 @@
     innr[...] = rhs(inner_ref[...], 1)
     own = table_ref[pl.ds(pl.multiple_of(j * 64, 64), 64), :]
     slope[...] = gelu_slope(dot3(own, inner_ref[...]))
-    for c in stat_cp:
+    for c in stat_cp[:7]:
         c.wait()
-    both = stats_all[0]
+    sums = stats_all[0, 0:8]
     for b in range(1, 8):
-        both = both + stats_all[b]
-    stats[...] = both
-    loss = jnp.log(stats[pl.ds(z, 1), :]) - stats[pl.ds(z + 8, 1), :]
-    loss_ref[...] = loss.reshape(256)
-    stats[0:8, :] = inverse_temp / both[0:8, :]
+        sums = sums + stats_all[b, 0:8]
+    stats_all[z, 0:8] = sums
+    stats[0:8, :] = inverse_temp / sums
 
     def coefficients(i, b):
         hit = pos_all[b][0:1, :] == numbers(i)
@@ -444,6 +447,12 @@
     dsend[1] = total[256:512]
     to_sib[1].start()
     q_step(1)
+    for c in stat_cp[7:]:
+        c.wait()
+    loss = jnp.log(stats_all[z, pl.ds(z, 1), :])
+    for b in range(8):
+        loss = loss - stats_all[b, pl.ds(z + 8, 1), :]
+    loss_ref[...] = loss.reshape(256)
     to_sib[1].wait_recv()
     mine = total[0:256] + dgot[1]
     across.wait_recv()
@@ -619,7 +628,7 @@
             DMA((2, 4)),
             DMA((2, 7)),
             DMA((2, 3)),
-            DMA((2, 7)),
+            DMA((2, 14)),
             DMA((2, 3)),
             DMA((2, 14)),
             DMA((2, 2)),

time: 137 us -> 136 us (level)
  no operation moved by 1% of the time
where the time goes in v5:
time: 136 us
  Pallas kernels  135 us (99%)
    pallas_call x1, Pallas kernels, per_device(): pl.pallas_call(step_kernel, name='step', out_shape=[jax.ShapeDtypeStruct(...  134 us

profile of v5, /device:TPU:1, one launch (start us, length us, event | category | flops | bytes accessed | tf_op | source)
XLA Modules:
  0.0 135.9 jit_solution(2754708869907839326)
XLA Ops:
  0.6 133.5 %step.1 = (f32[256]{0:T(256)}, f32[256,256]{1,0:T(8,128)}, f32[64,256]{1,0:T(8,128)}) custom-call(s32[8,256]{1,0:T(8,128)} %bitcast.5, s32[8]{0:T(128)} %bitcast.7, s32[8,512]{1,0:T(8,128)} %bitcast.4, s32[1,256]{1,0:T(1,128)} %bitcast.6, f32[2048,256]{1,0:T(8,128)} %table_hbm.1, f32[256,512]{1,0:T(8,128)} %inner_hbm.1, f32[512,256]{1,0:T(8,128)} %outer_hbm.1, ...), custom_call_target="tpu_custom_call" | custom-call | tf_op jit(solution)/shard_map/step/pallas_call | solution.py:572
  134.2 1.7 %keep.1 = (f32[256]{0:T(256)}, f32[256,256]{1,0:T(8,128)}, f32[64,256]{1,0:T(8,128)}) custom-call(f32[256]{0:T(256)} %get-tuple-element.6.a_ref, f32[256,256]{1,0:T(8,128)} %get-tuple-element.7.b_ref, f32[64,256]{1,0:T(8,128)} %get-tuple-element.8.c_ref), custom_call_target="tpu_custom_call" | custom-call | tf_op jit(solution)/shard_map/keep/pallas_call | solution.py:653
